TPU v7x, 32 devices: a whole 2x2x4 slice. The times are simulated.
32 devices in a mesh: dp: 16 (over z, y, core), seq: 2 (over x).
Axes of the slice: x: 2, y: 2, z: 4, core: 2. Of those that a mesh axis runs over, the one named last changes fastest.
Arguments:
- activations: bfloat16 [16, 1024, 1152], P('dp', 'seq'), may hold values from -6 to 6
- conditioning: bfloat16 [16, 1152], P('dp'), may hold values from -6 to 6
- cotangent: bfloat16 [16, 1024, 1152], P('dp', 'seq'), may hold values from -6 to 6
- w_ada: bfloat16 [7962624], P(('dp', 'seq')), may hold values from -0.1875 to 0.1875
- b_ada: bfloat16 [6912], P(('dp', 'seq')), may hold values from -3 to 3
- w_query: bfloat16 [1327104], P(('dp', 'seq')), may hold values from -0.1875 to 0.1875
- w_key: bfloat16 [1327104], P(('dp', 'seq')), may hold values from -0.1875 to 0.1875
- w_value: bfloat16 [1327104], P(('dp', 'seq')), may hold values from -0.1875 to 0.1875
- w_forget: bfloat16 [18432], P(('dp', 'seq')), may hold values from -0.1875 to 0.1875
- b_forget: bfloat16 [16], replicated, may hold values from -8 to -3
- conv_taps: bfloat16 [11520], P(('dp', 'seq')), may hold values from -2 to 2
- w_out: bfloat16 [1327104], P(('dp', 'seq')), may hold values from -0.1875 to 0.1875
- w_up: bfloat16 [5308416], P(('dp', 'seq')), may hold values from -0.1875 to 0.1875
- w_down: bfloat16 [5308416], P(('dp', 'seq')), may hold values from -0.09375 to 0.09375
Outputs:
- output: bfloat16 [16, 1024, 1152], P('dp', 'seq')
- grad_input: float32 [16, 1024, 1152], P('dp', 'seq')
- grad_ada: float32 [7962624], P(('dp', 'seq'))
- grad_ada_bias: float32 [6912], P(('dp', 'seq'))
- grad_query: float32 [1327104], P(('dp', 'seq'))
- grad_key: float32 [1327104], P(('dp', 'seq'))
- grad_value: float32 [1327104], P(('dp', 'seq'))
- grad_forget: float32 [18432], P(('dp', 'seq'))
- grad_forget_bias: float32 [16], replicated
- grad_conv: float32 [11520], P(('dp', 'seq'))
- grad_out: float32 [1327104], P(('dp', 'seq'))
- grad_up: float32 [5308416], P(('dp', 'seq'))
- grad_down: float32 [5308416], P(('dp', 'seq'))
All inputs are finite; a program needn't handle non-finite values.
Results may differ from a plain program's by a relative error of at most 0.022.
The roundings to bfloat16 on the way count: a program that leaves them out, or rounds other values in their place, can miss the bound.
Values may be sent and summed in bfloat16 or wider, within the bound.
A program may use at most 448 MiB of HBM per device.

v0:
```python
import jax
import jax.numpy as jnp
from jax import lax
from jax.sharding import PartitionSpec as P

GRID = 32
GROUP = 64


epsilon = 1e-06
highest = lax.Precision.HIGHEST


def carried_in(value, axis, join, neutral, backward):
    count = lax.axis_size(axis)
    place = lax.axis_index(axis)
    ahead = count - 1 - place if backward else place
    gathered = jax.tree.map(
        lambda a, kind: lax.all_gather(a.astype(kind), axis),
        value,
        jax.tree.map(lambda a: jnp.bfloat16 if a.dtype == jnp.float32 else a.dtype, value),
    )
    state = jax.tree.map(lambda a, e: jnp.zeros_like(a) + jnp.asarray(e, a.dtype), value, neutral)

    def one(lap, state):
        source = count - 1 - lap if backward else lap
        return join(
            state,
            jax.tree.map(
                lambda a, own: lax.dynamic_index_in_dim(a, source, 0, False).astype(own.dtype),
                gathered,
                value,
            ),
        )

    return lax.fori_loop(0, ahead, one, state)


def with_halo(block, sides, width):
    for axis, dim in sides:
        count = lax.axis_size(axis)
        forward = [(i, i + 1) for i in range(count - 1)]
        backward = [(target, source) for source, target in forward]
        low = lax.ppermute(
            lax.slice_in_dim(block, block.shape[dim] - width, None, axis=dim), axis, forward
        )
        high = lax.ppermute(lax.slice_in_dim(block, 0, width, axis=dim), axis, backward)
        block = jnp.concatenate([low, block, high], axis=dim)
    return block


def layer_norm(values, offset, factor):
    center = jnp.mean(values, axis=-1, keepdims=True)
    centered = values - center
    spread = jnp.mean(centered * centered, axis=-1, keepdims=True)
    return centered * lax.rsqrt(spread + epsilon) * (1.0 + factor) + offset


def head_norm(mixture):
    mean_square = jnp.mean(mixture * mixture, axis=-1, keepdims=True)
    return mixture * lax.rsqrt(mean_square + epsilon)


def gelu_tanh(values):
    return jax.nn.gelu(values, approximate=True)


def times_transpose(rows, matrix):
    return lax.dot_general(
        rows, matrix, (((1,), (1,)), ((), ())), preferred_element_type=jnp.float32
    )


def group_scan(queries, key_rows, values, logdecay, opening):
    length = queries.shape[0]
    blocks_total = length // GROUP
    causal = (jnp.arange(GROUP)[:, None] >= jnp.arange(GROUP)[None, :])[:, :, None]

    def advance(carried, pieces):
        q_part, k_part, v_part, g_part = pieces
        running = jnp.cumsum(g_part, axis=0)
        spread = jnp.where(causal, running[:, None, :] - running[None, :, :], 0.0)
        weight = jnp.where(causal, jnp.exp(spread), 0.0)
        scores = jnp.einsum("the,she->tsh", q_part, k_part, precision=highest) * weight
        within = jnp.einsum("tsh,shf->thf", scores, v_part, precision=highest)
        earlier = jnp.exp(running)[:, :, None] * jnp.einsum(
            "the,hef->thf", q_part, carried, precision=highest
        )
        remaining = jnp.exp(running[-1][None, :] - running)
        update = jnp.einsum(
            "she,shf->hef", k_part * remaining[:, :, None], v_part, precision=highest
        )
        return (jnp.exp(running[-1])[:, None, None] * carried + update, within + earlier)

    pieces = tuple(
        (
            source.reshape((blocks_total, GROUP) + source.shape[1:])
            for source in (queries, key_rows, values, logdecay)
        )
    )
    closing, outputs = lax.scan(jax.checkpoint(advance), opening, pieces)
    return (outputs.reshape(queries.shape), closing)


def local_pass(queries, key_rows, values, logdecay, incoming):
    outputs, closing = group_scan(queries, key_rows, values, logdecay, jnp.zeros_like(incoming))
    running = jnp.cumsum(logdecay, axis=0)
    carried = jnp.einsum("the,hef->thf", queries, incoming, precision=highest)
    return (
        outputs + jnp.exp(running)[:, :, None] * carried,
        closing + jnp.exp(running[-1])[:, None, None] * incoming,
    )


def depthwise(padded, kernel):
    height = padded.shape[1] - 2
    across = padded.shape[2]
    widened = jnp.pad(padded, ((0, 0), (0, 0), (1, 1), (0, 0)))
    summed = jnp.zeros((padded.shape[0], height, across, padded.shape[3]), jnp.float32)
    for vertical in range(3):
        for lateral in range(3):
            window = widened[:, vertical : vertical + height, lateral : lateral + across].astype(
                jnp.float32
            )
            summed = summed + kernel[3 * vertical + lateral] * window
    return summed


def join_states(earlier, latter):
    return (earlier[0] * latter[0], latter[0][..., None, None] * earlier[1] + latter[1])


def states_rising(decays, summary):
    neutral = (jnp.ones_like(decays), jnp.zeros_like(summary))
    return carried_in((decays, summary), "seq", join_states, neutral, False)[1]


def states_falling(decays, summary):
    neutral = (jnp.ones_like(decays), jnp.zeros_like(summary))
    return carried_in((decays, summary), "seq", join_states, neutral, True)[1]


def grid_rims(grid_block):
    return with_halo(grid_block, (("seq", 1),), 1)


def direction_forward(queries, key_rows, values, logdecay, rising):
    opening = jnp.zeros(
        (queries.shape[0], queries.shape[2], queries.shape[3], queries.shape[3]), jnp.float32
    )
    outputs, closing = jax.vmap(group_scan)(queries, key_rows, values, logdecay, opening)
    running = jnp.cumsum(logdecay, axis=1)
    decays = jnp.exp(running[:, -1])
    incoming = states_rising(decays, closing) if rising else states_falling(decays, closing)
    carried = jnp.einsum("ithe,ihef->ithf", queries, incoming, precision=highest)
    return (outputs + jnp.exp(running)[..., None] * carried, incoming)


def direction_backward(queries, key_rows, values, logdecay, incoming, grad_mix, rising):
    running = jnp.cumsum(logdecay, axis=1)
    decays = jnp.exp(running[:, -1])
    summary = jnp.einsum(
        "ithe,ithf->ihef", queries * jnp.exp(running)[..., None], grad_mix, precision=highest
    )
    leaving = states_falling(decays, summary) if rising else states_rising(decays, summary)
    _, pullback = jax.vjp(jax.vmap(local_pass), queries, key_rows, values, logdecay, incoming)
    return pullback((grad_mix, leaving))[:4]


def unpack(gathered, model_width, head_count):
    (
        ada_flat,
        ada_bias,
        query_flat,
        key_flat,
        value_flat,
        forget_flat,
        conv_flat,
        out_flat,
        up_flat,
        down_flat,
    ) = gathered
    hidden_width = up_flat.shape[0] // model_width
    return (
        ada_flat.reshape(model_width, 6 * model_width),
        ada_bias,
        query_flat.reshape(model_width, model_width),
        key_flat.reshape(model_width, model_width),
        value_flat.reshape(model_width, model_width),
        forget_flat.reshape(model_width, head_count),
        conv_flat.reshape(10, model_width),
        out_flat.reshape(model_width, model_width),
        up_flat.reshape(model_width, hidden_width),
        down_flat.reshape(hidden_width, model_width),
    )


def on_device(
    activations,
    conditioning,
    cotangent,
    w_ada,
    b_ada,
    w_query,
    w_key,
    w_value,
    w_forget,
    b_forget,
    conv_taps,
    w_out,
    w_up,
    w_down,
):
    images, length, model_width = activations.shape
    head_count = b_forget.shape[0]
    head_width = model_width // head_count
    grid_height = length // GRID
    data_count = lax.axis_size("dp")
    seq_count = lax.axis_size("seq")

    def sectioned(flat):
        return flat.reshape(data_count, seq_count, -1)

    shards = (w_ada, b_ada, w_query, w_key, w_value, w_forget, conv_taps, w_out, w_up, w_down)
    gathered = (
        lax.all_gather(shards[0], ("dp", "seq"), axis=0, tiled=True),
        lax.all_gather(shards[1], ("dp", "seq"), axis=0, tiled=True),
        lax.all_gather(shards[2], ("dp", "seq"), axis=0, tiled=True),
        lax.all_gather(shards[3], ("dp", "seq"), axis=0, tiled=True),
        lax.all_gather(shards[4], ("dp", "seq"), axis=0, tiled=True),
        lax.all_gather(shards[5], ("dp", "seq"), axis=0, tiled=True),
        lax.all_gather(shards[6], ("dp", "seq"), axis=0, tiled=True),
        lax.all_gather(shards[7], ("dp", "seq"), axis=0, tiled=True),
        lax.all_gather(shards[8], ("dp", "seq"), axis=0, tiled=True),
        lax.all_gather(shards[9], ("dp", "seq"), axis=0, tiled=True),
    )
    forward_weights = unpack(gathered, model_width, head_count)
    ada_matrix, ada_bias, query_w, key_w, value_w, forget_w, conv_w, out_w, up_w, down_w = (
        forward_weights
    )
    cond_act = jax.nn.silu(conditioning.astype(jnp.float32)).astype(jnp.bfloat16)
    modulation = jnp.dot(
        cond_act, ada_matrix, preferred_element_type=jnp.float32
    ) + ada_bias.astype(jnp.float32)
    pieces = modulation.reshape(images, 6, 1, model_width)
    shift_one, scale_one, gate_one, shift_two, scale_two, gate_two = [
        pieces[:, position] for position in range(6)
    ]
    inputs = activations.astype(jnp.float32)
    pre_one, norm_one_pull = jax.vjp(layer_norm, inputs, shift_one, scale_one)
    hidden_one = pre_one.astype(jnp.bfloat16).reshape(-1, model_width)

    def project(matrix):
        return jnp.dot(hidden_one, matrix, preferred_element_type=jnp.float32)

    queries = project(query_w).astype(jnp.bfloat16)
    key_rows = project(key_w).astype(jnp.bfloat16)
    values = project(value_w).astype(jnp.bfloat16)
    gate_pre = project(forget_w) + b_forget.astype(jnp.float32)
    logdecay = (-jax.nn.softplus(gate_pre)).reshape(images, length, head_count)

    def split_heads(matrix):
        return matrix.astype(jnp.float32).reshape(images, length, head_count, head_width)

    def reverse_rows(tensor):
        return jnp.flip(tensor, axis=1)

    query_f, key_f, value_f = (split_heads(queries), split_heads(key_rows), split_heads(values))
    forward_mix, incoming_up = direction_forward(query_f, key_f, value_f, logdecay, True)
    behind, incoming_down = direction_forward(
        reverse_rows(query_f),
        reverse_rows(key_f),
        reverse_rows(value_f),
        reverse_rows(logdecay),
        False,
    )
    normed, head_pull = jax.vjp(head_norm, forward_mix + reverse_rows(behind))
    value_rims = grid_rims(values.reshape(images, grid_height, GRID, model_width))
    conv_kernel = conv_w[:9].astype(jnp.float32)
    conv_bias = conv_w[9].astype(jnp.float32)
    conv_out = depthwise(value_rims, conv_kernel).reshape(images, length, model_width)
    mixed = (
        (normed.reshape(images, length, model_width) + conv_out + conv_bias)
        .astype(jnp.bfloat16)
        .reshape(-1, model_width)
    )
    branch = jnp.dot(mixed, out_w, preferred_element_type=jnp.float32).reshape(
        images, length, model_width
    )
    middle = inputs + gate_one * branch
    pre_two, norm_two_pull = jax.vjp(layer_norm, middle, shift_two, scale_two)
    hidden_two = pre_two.astype(jnp.bfloat16).reshape(-1, model_width)
    up_pre = jnp.dot(hidden_two, up_w, preferred_element_type=jnp.float32)
    activated, gelu_pull = jax.vjp(gelu_tanh, up_pre)
    activated = activated.astype(jnp.bfloat16)
    down_out = jnp.dot(activated, down_w, preferred_element_type=jnp.float32).reshape(
        images, length, model_width
    )
    output = (middle + gate_two * down_out).astype(jnp.bfloat16)
    weights_back = unpack(
        (
            lax.all_gather(shards[0], ("dp", "seq"), axis=0, tiled=True),
            lax.all_gather(shards[1], ("dp", "seq"), axis=0, tiled=True),
            lax.all_gather(shards[2], ("dp", "seq"), axis=0, tiled=True),
            lax.all_gather(shards[3], ("dp", "seq"), axis=0, tiled=True),
            lax.all_gather(shards[4], ("dp", "seq"), axis=0, tiled=True),
            lax.all_gather(shards[5], ("dp", "seq"), axis=0, tiled=True),
            lax.all_gather(shards[6], ("dp", "seq"), axis=0, tiled=True),
            lax.all_gather(shards[7], ("dp", "seq"), axis=0, tiled=True),
            lax.all_gather(shards[8], ("dp", "seq"), axis=0, tiled=True),
            lax.all_gather(shards[9], ("dp", "seq"), axis=0, tiled=True),
        ),
        model_width,
        head_count,
    )
    query_back, key_back, value_back, forget_back = (
        weights_back[2],
        weights_back[3],
        weights_back[4],
        weights_back[5],
    )
    out_back, up_back, down_back = (weights_back[7], weights_back[8], weights_back[9])
    grad_final = cotangent.astype(jnp.float32)
    grad_down_in = (grad_final * gate_two).astype(jnp.bfloat16).reshape(-1, model_width)
    grad_gate_two = jnp.sum(grad_final * down_out, axis=1, keepdims=True)
    grad_down = jnp.einsum("nf,nd->fd", activated, grad_down_in, preferred_element_type=jnp.float32)
    grad_act = times_transpose(grad_down_in, down_back)
    grad_up_in = gelu_pull(grad_act)[0].astype(jnp.bfloat16)
    grad_up = jnp.einsum("nd,nf->df", hidden_two, grad_up_in, preferred_element_type=jnp.float32)
    grad_hidden_two = times_transpose(grad_up_in, up_back).reshape(images, length, model_width)
    mlp_part = (
        lax.psum_scatter(
            sectioned(grad_up.reshape(-1)).astype(jnp.bfloat16),
            "seq",
            scatter_dimension=1,
            tiled=True,
        ).astype(jnp.float32),
        lax.psum_scatter(
            sectioned(grad_down.reshape(-1)).astype(jnp.bfloat16),
            "seq",
            scatter_dimension=1,
            tiled=True,
        ).astype(jnp.float32),
    )
    mlp_whole = (
        lax.psum_scatter(
            mlp_part[0].astype(jnp.bfloat16), "dp", scatter_dimension=0, tiled=True
        ).astype(jnp.float32),
        lax.psum_scatter(
            mlp_part[1].astype(jnp.bfloat16), "dp", scatter_dimension=0, tiled=True
        ).astype(jnp.float32),
    )
    grad_up_shard = mlp_whole[0].reshape(-1)
    grad_down_shard = mlp_whole[1].reshape(-1)
    grad_middle_norm, grad_shift_two, grad_scale_two = norm_two_pull(grad_hidden_two)
    grad_middle = grad_final + grad_middle_norm
    grad_branch = (grad_middle * gate_one).astype(jnp.bfloat16).reshape(-1, model_width)
    grad_gate_one = jnp.sum(grad_middle * branch, axis=1, keepdims=True)
    grad_out = jnp.einsum("nd,ne->de", mixed, grad_branch, preferred_element_type=jnp.float32)
    grad_mixed = times_transpose(grad_branch, out_back).astype(jnp.bfloat16)
    grad_mixed = grad_mixed.reshape(images, grid_height, GRID, model_width)
    grad_rims = grid_rims(grad_mixed)
    grad_conv_value = depthwise(grad_rims, conv_kernel[::-1]).reshape(images, length, model_width)
    widened = jnp.pad(value_rims, ((0, 0), (0, 0), (1, 1), (0, 0)))
    grad_mixed_f = grad_mixed.astype(jnp.float32)
    kernel_rows = []
    for vertical in range(3):
        for lateral in range(3):
            window = widened[:, vertical : vertical + grid_height, lateral : lateral + GRID].astype(
                jnp.float32
            )
            kernel_rows.append(jnp.sum(window * grad_mixed_f, axis=(0, 1, 2)))
    kernel_rows.append(jnp.sum(grad_mixed_f, axis=(0, 1, 2)))
    grad_conv = jnp.stack(kernel_rows)
    grad_mix = head_pull(grad_mixed_f.reshape(images, length, head_count, head_width))[0]
    grads_ahead = direction_backward(query_f, key_f, value_f, logdecay, incoming_up, grad_mix, True)
    grads_behind = direction_backward(
        reverse_rows(query_f),
        reverse_rows(key_f),
        reverse_rows(value_f),
        reverse_rows(logdecay),
        incoming_down,
        reverse_rows(grad_mix),
        False,
    )
    grad_q = (
        (grads_ahead[0] + reverse_rows(grads_behind[0]))
        .astype(jnp.bfloat16)
        .reshape(-1, model_width)
    )
    grad_k = (
        (grads_ahead[1] + reverse_rows(grads_behind[1]))
        .astype(jnp.bfloat16)
        .reshape(-1, model_width)
    )
    grad_v_heads = (grads_ahead[2] + reverse_rows(grads_behind[2])).reshape(
        images, length, model_width
    )
    grad_v = (grad_v_heads + grad_conv_value).astype(jnp.bfloat16).reshape(-1, model_width)
    grad_logdecay = (grads_ahead[3] + reverse_rows(grads_behind[3])).reshape(-1, head_count)
    grad_gate = (-grad_logdecay * jax.nn.sigmoid(gate_pre)).astype(jnp.bfloat16)

    def weight_grad(grad_rows):
        return jnp.einsum("nd,ne->de", hidden_one, grad_rows, preferred_element_type=jnp.float32)

    grad_query = weight_grad(grad_q)
    grad_key = weight_grad(grad_k)
    grad_value = weight_grad(grad_v)
    grad_forget = weight_grad(grad_gate)
    grad_forget_bias = lax.psum(jnp.sum(grad_gate.astype(jnp.float32), axis=0), ("dp", "seq"))
    grad_hidden_one = (
        times_transpose(grad_q, query_back)
        + times_transpose(grad_k, key_back)
        + times_transpose(grad_v, value_back)
        + times_transpose(grad_gate, forget_back)
    )
    grad_inputs_norm, grad_shift_one, grad_scale_one = norm_one_pull(
        grad_hidden_one.reshape(images, length, model_width)
    )
    grad_input = grad_middle + grad_inputs_norm
    grad_mod = jnp.concatenate(
        [
            grad_shift_one,
            grad_scale_one,
            grad_gate_one,
            grad_shift_two,
            grad_scale_two,
            grad_gate_two,
        ],
        axis=1,
    ).reshape(images, 6 * model_width)
    grad_ada = jnp.dot(cond_act.astype(jnp.float32).T, grad_mod, precision=highest)
    grad_ada_bias = jnp.sum(grad_mod, axis=0)
    parted = (
        lax.psum_scatter(
            sectioned(grad_ada.reshape(-1)).astype(jnp.bfloat16),
            "seq",
            scatter_dimension=1,
            tiled=True,
        ).astype(jnp.float32),
        lax.psum_scatter(
            sectioned(grad_ada_bias).astype(jnp.bfloat16), "seq", scatter_dimension=1, tiled=True
        ).astype(jnp.float32),
        lax.psum_scatter(
            sectioned(grad_query.reshape(-1)).astype(jnp.bfloat16),
            "seq",
            scatter_dimension=1,
            tiled=True,
        ).astype(jnp.float32),
        lax.psum_scatter(
            sectioned(grad_key.reshape(-1)).astype(jnp.bfloat16),
            "seq",
            scatter_dimension=1,
            tiled=True,
        ).astype(jnp.float32),
        lax.psum_scatter(
            sectioned(grad_value.reshape(-1)).astype(jnp.bfloat16),
            "seq",
            scatter_dimension=1,
            tiled=True,
        ).astype(jnp.float32),
        lax.psum_scatter(
            sectioned(grad_forget.reshape(-1)).astype(jnp.bfloat16),
            "seq",
            scatter_dimension=1,
            tiled=True,
        ).astype(jnp.float32),
        lax.psum_scatter(
            sectioned(grad_conv.reshape(-1)).astype(jnp.bfloat16),
            "seq",
            scatter_dimension=1,
            tiled=True,
        ).astype(jnp.float32),
        lax.psum_scatter(
            sectioned(grad_out.reshape(-1)).astype(jnp.bfloat16),
            "seq",
            scatter_dimension=1,
            tiled=True,
        ).astype(jnp.float32),
    )
    summed = (
        lax.psum_scatter(
            parted[0].astype(jnp.bfloat16), "dp", scatter_dimension=0, tiled=True
        ).astype(jnp.float32),
        lax.psum_scatter(
            parted[1].astype(jnp.bfloat16), "dp", scatter_dimension=0, tiled=True
        ).astype(jnp.float32),
        lax.psum_scatter(
            parted[2].astype(jnp.bfloat16), "dp", scatter_dimension=0, tiled=True
        ).astype(jnp.float32),
        lax.psum_scatter(
            parted[3].astype(jnp.bfloat16), "dp", scatter_dimension=0, tiled=True
        ).astype(jnp.float32),
        lax.psum_scatter(
            parted[4].astype(jnp.bfloat16), "dp", scatter_dimension=0, tiled=True
        ).astype(jnp.float32),
        lax.psum_scatter(
            parted[5].astype(jnp.bfloat16), "dp", scatter_dimension=0, tiled=True
        ).astype(jnp.float32),
        lax.psum_scatter(
            parted[6].astype(jnp.bfloat16), "dp", scatter_dimension=0, tiled=True
        ).astype(jnp.float32),
        lax.psum_scatter(
            parted[7].astype(jnp.bfloat16), "dp", scatter_dimension=0, tiled=True
        ).astype(jnp.float32),
    )
    shares = [member.reshape(-1) for member in summed]
    return (
        output,
        grad_input,
        shares[0],
        shares[1],
        shares[2],
        shares[3],
        shares[4],
        shares[5],
        grad_forget_bias,
        shares[6],
        shares[7],
        grad_up_shard,
        grad_down_shard,
    )


def solution(mesh):
    return jax.shard_map(
        on_device,
        mesh=mesh,
        in_specs=(
            P("dp", "seq", None),
            P("dp", None),
            P("dp", "seq", None),
            P(("dp", "seq")),
            P(("dp", "seq")),
            P(("dp", "seq")),
            P(("dp", "seq")),
            P(("dp", "seq")),
            P(("dp", "seq")),
            P(),
            P(("dp", "seq")),
            P(("dp", "seq")),
            P(("dp", "seq")),
            P(("dp", "seq")),
        ),
        out_specs=(
            P("dp", "seq", None),
            P("dp", "seq", None),
            P(("dp", "seq")),
            P(("dp", "seq")),
            P(("dp", "seq")),
            P(("dp", "seq")),
            P(("dp", "seq")),
            P(("dp", "seq")),
            P(),
            P(("dp", "seq")),
            P(("dp", "seq")),
            P(("dp", "seq")),
            P(("dp", "seq")),
        ),
        check_vma=False,
    )
```

profile of v0, /device:TPU:0, one launch (start us, length us, event | category | flops | bytes accessed | tf_op | source)
XLA Modules:
  0.0 3348.4 jit_solution(12469606696391647413)
XLA Ops:
  22.6 115.4 %all-reduce.29.cloned.1.call-done = (bf16[6912]{0:T(1024)(128)(2,1)}, bf16[11520]{0:T(1024)(128)(2,1)}, bf16[18432]{0:T(1024)(128)(2,1)}) async-done(((bf16[6912]{0:T(1024)(128)(2,1)}, bf16[11520]{0:T(1024)(128)(2,1)}, bf16[18432]{0:T(1024)(128)(2,1)}), (bf16[6912]{0:T(1024)(128)(2,1)}, bf16[11520]{0:T(1024)(128)(2,1)}, bf16[18432]{0:T(1024)(128)(2,1)})) %all-reduce.29.cloned.1.call-update) | async-done | bytes 73744
  142.5 66.7 %all-gather.24.cloned.1.call-done = bf16[32,1,41472]{2,1,0:T(2,128)(2,1)} async-done(((bf16[1,1,41472]{2,1,0:T(2,128)(2,1)}), bf16[32,1,41472]{2,1,0:T(2,128)(2,1)}) %all-gather.24.cloned.1.call-update) | async-done | bytes 2654224 | tf_op jit(solution)/shard_map/all_gather | solution.py:230
  209.1 49.1 %reduce.116 = bf16[32,41472]{1,0:T(8,128)(2,1)} reduce(bf16[32,1,41472]{2,1,0:T(2,128)(2,1)} %all-gather.24.cloned.1.call-done, bf16[]{:T(256)} %constant.391), dimensions={1}, to_apply=%all-gather.5.reduce_sub_computation | reduce | bytes 5308418 | tf_op jit(solution)/shard_map/all_gather | solution.py:230
  277.2 48.6 %reduce.115 = bf16[32,41472]{1,0:T(8,128)(2,1)} reduce(bf16[32,1,41472]{2,1,0:T(2,128)(2,1)} %all-gather.22.cloned.1.call-done, bf16[]{:T(256)} %constant.391), dimensions={1}, to_apply=%all-gather.4.reduce_sub_computation | reduce | bytes 5308418 | tf_op jit(solution)/shard_map/all_gather | solution.py:229
  345.2 48.7 %reduce.117 = bf16[32,41472]{1,0:T(8,128)(2,1)} reduce(bf16[32,1,41472]{2,1,0:T(2,128)(2,1)} %all-gather.26.cloned.1.call-done, bf16[]{:T(256)} %constant.391), dimensions={1}, to_apply=%all-gather.6.reduce_sub_computation | reduce | bytes 5308418 | tf_op jit(solution)/shard_map/all_gather | solution.py:228
  413.1 48.6 %reduce.120 = bf16[32,41472]{1,0:T(8,128)(2,1)} reduce(bf16[32,1,41472]{2,1,0:T(2,128)(2,1)} %all-gather.28.cloned.1.call-done, bf16[]{:T(256)} %constant.391), dimensions={1}, to_apply=%all-gather.7.reduce_sub_computation | reduce | bytes 5308418 | tf_op jit(solution)/shard_map/all_gather | solution.py:233
  468.1 34.1 %all-gather.18.cloned.1.call-done = bf16[5308416]{0:T(1024)(128)(2,1)} async-done(((bf16[165888]{0:T(1024)(128)(2,1)}), bf16[5308416]{0:T(1024)(128)(2,1)}) %all-gather.18.cloned.1.call-update) | async-done | bytes 10616848 | tf_op jit(solution)/shard_map/all_gather | solution.py:234
  502.2 19.3 reshape.2284
  521.5 69.4 %all-gather.20.cloned.1.call-done = bf16[5308416]{0:T(1024)(128)(2,1)} async-done(((bf16[165888]{0:T(1024)(128)(2,1)}), bf16[5308416]{0:T(1024)(128)(2,1)}) %all-gather.20.cloned.1.call-update) | async-done | bytes 10616848 | tf_op jit(solution)/shard_map/all_gather | solution.py:235
  590.9 20.4 reshape.2285
  611.3 92.0 %all-gather.16.cloned.1.call-done = bf16[7962624]{0:T(1024)(128)(2,1)} async-done(((bf16[248832]{0:T(1024)(128)(2,1)}), bf16[7962624]{0:T(1024)(128)(2,1)}) %all-gather.16.cloned.1.call-update) | async-done | bytes 15925264 | tf_op jit(solution)/shard_map/all_gather | solution.py:226
  703.3 29.0 reshape.2251
  808.2 32.2 rev.37
  850.3 32.1 rev.38
  892.5 32.2 rev.39
  937.2 85.2 %while.161 = (s32[]{:T(128)}, f32[1,16,72,72]{3,2,1,0:T(8,128)S(1)}, f32[8,1,64,16,72]{4,2,3,1,0:T(8,128)}, f32[8,1,64,16]{3,2,1,0:T(8,128)}, f32[8,1,64,16,72]{...) while((s32[]{:T(128)}, f32[1,16,72,72]{3,2,1,0:T(8,128)S(1)}, ...), condition=%wide.region_11.12_spmd.clone.clone, body=%wide.region_9.11_spmd.clone.clone.sunk | while | flops 241532928 | bytes 5857794 | solution.py:101
  1053.7 32.2 rev.41
  1100.5 85.3 %while.160 = (s32[]{:T(128)}, f32[1,16,72,72]{3,2,1,0:T(8,128)S(1)}, f32[8,1,64,16,72]{4,2,3,1,0:T(8,128)}, f32[8,1,64,16]{3,2,1,0:T(8,128)}, f32[8,1,64,16,72]{...) while((s32[]{:T(128)}, f32[1,16,72,72]{3,2,1,0:T(8,128)S(1)}, ...), condition=%wide.region_4.5_spmd.clone.clone, body=%wide.region_2.4_spmd.clone.clone.sunk | while | flops 241532928 | bytes 5857794 | solution.py:101
  1211.5 37.8 %while.159 = (s32[]{:T(128)}, f32[1,16,72,72]{3,2,1,0:T(8,128)S(1)}, f32[8,1,16,72,72]{4,3,2,1,0:T(8,128)}, f32[8,1,64,16]{3,2,1,0:T(8,128)}, f32[8,1,64,16,72]{...) while((s32[]{:T(128)}, f32[1,16,72,72]{3,2,1,0:T(8,128)S(1)}, ...), condition=%wide.region_41.42_spmd.clone, body=%wide.region_39.41_spmd.clone.sunk | while | flops 64172032 | bytes 2672635 | solution.py:101
  1251.9 37.5 %while.158 = (s32[]{:T(128)}, f32[1,16,72,72]{3,2,1,0:T(8,128)S(1)}, f32[8,1,16,72,72]{4,3,2,1,0:T(8,128)}, f32[8,1,64,16]{3,2,1,0:T(8,128)}, f32[8,1,64,16,72]{...) while((s32[]{:T(128)}, f32[1,16,72,72]{3,2,1,0:T(8,128)S(1)}, ...), condition=%wide.region_26.27_spmd.clone, body=%wide.region_24.26_spmd.clone.sunk | while | flops 64172032 | bytes 2672635 | solution.py:101
  1377.1 22.6 rev.42
  1525.5 164.2 %while.157 = (s32[]{:T(128)}, f32[1,16,72,72]{2,3,1,0:T(8,128)S(1)}, f32[8,1,64,16,72]{4,2,3,1,0:T(8,128)}, f32[8,1,64,16,72]{4,2,3,1,0:T(8,128)}, f32[8,1,64,16...) while((s32[]{:T(128)}, f32[1,16,72,72]{2,3,1,0:T(8,128)S(1)}, ...), condition=%wide.region_51.52_spmd.clone, body=%wide.region_42.51_spmd.clone.sunk | while | flops 604216320 | bytes 21648476 | solution.py:101
  1698.1 163.2 %while.156 = (s32[]{:T(128)}, f32[1,16,72,72]{2,3,1,0:T(8,128)S(1)}, f32[8,1,64,16,72]{4,2,3,1,0:T(8,128)}, f32[8,1,64,16,72]{4,2,3,1,0:T(8,128)}, f32[8,1,64,16...) while((s32[]{:T(128)}, f32[1,16,72,72]{2,3,1,0:T(8,128)S(1)}, ...), condition=%wide.region_36.37_spmd.clone, body=%wide.region_27.36_spmd.clone.sunk | while | flops 604216320 | bytes 19289124 | solution.py:101
  1879.1 32.2 rev.43
  1942.5 32.2 rev.44
  2057.0 32.2 rev.45
  2203.3 18.2 convert_element_type.514
  2259.0 38.2 %psum.7 = f32[16]{0:T(128)} all-reduce(f32[16]{0:T(128)S(1)} %copy-done.129), channel_id=1, replica_groups=mesh['dp'=16,'seq'=2] {'dp','seq'}, use_global_device_ids=true, to_apply=%region_81.82 | all-reduce | flops 16 | bytes 128 | tf_op jit(solution)/shard_map/psum | solution.py:410
  2299.5 61.3 %all-reduce.22 = (bf16[16,1,216]{2,1,0:T(2,128)(2,1)S(1)}, bf16[16,1,576]{2,1,0:T(2,128)(2,1)S(1)}, bf16[16,1,360]{2,1,0:T(2,128)(2,1)S(1)}) all-reduce(bf16[16,1,216]{2,1,0:T(2,128)(2,1)S(1)} %copy.700, bf16[16,1,576]{2,1,0:T(2,128)(2,1)S(1)} %copy.709, ...), channel_id=9, replica_groups=mesh['dp'=16,'seq'=2] {'dp'}, use_global_device_ids=true, to_apply=%region_71.72.clone | all-reduce | flops 18432 | bytes 73728
  2384.3 109.0 %reduce-scatter.11.cloned.1.call-done = bf16[16,1,248832]{2,0,1:T(8,128)(2,1)} async-done(((bf16[16,2,248832]{2,0,1:T(8,128)(2,1)}), bf16[16,1,248832]{2,0,1:T(8,128)(2,1)}) %reduce-scatter.11.cloned.1.call-update) | async-done | bytes 7962640 | tf_op jit(solution)/shard_map/reduce_scatter | solution.py:435
  2508.5 355.7 %all-reduce.33.cloned.1.call-done = (bf16[16,1,165888]{2,1,0:T(2,128)(2,1)}, bf16[16,1,165888]{2,1,0:T(2,128)(2,1)}) async-done(((bf16[16,1,165888]{2,1,0:T(2,128)(2,1)}, bf16[16,1,165888]{2,1,0:T(2,128)(2,1)}), (bf16[16,1,165888]{2,1,0:T(2,128)(2,1)}, bf16[16,1,165888]{2,1,0:T(2,128)(2,1)})) %all-reduce.33.cloned.1.call-update) | async-done | bytes 10616848
  2868.2 463.0 %all-reduce.31.cloned.1.call-done = (bf16[16,1,248832]{2,1,0:T(2,128)(2,1)}, bf16[16,1,41472]{2,1,0:T(2,128)(2,1)}, bf16[16,1,41472]{2,1,0:T(2,128)(2,1)}, bf16[...) async-done(((bf16[16,1,248832]{2,1,0:T(2,128)(2,1)}, bf16[16,1,41472]{2,1,0:T(2,128)(2,1)}, bf16[16,1,41472]{2,1,0:T(2,128)(2,1)}, bf16[16,1,41472]{2,1,0:T(2,128)(2,1)}, ...) | async-done | bytes 13271056
  (1440 shorter events, 1394.1 us)
Async XLA Ops:
  7.2 130.8 %all-reduce.29.cloned.1.call-start = ((), (), s32[]{:S(2)}) async-start(), calls=%async_computation.27 | async-start | bytes 151552
  10.6 198.5 %all-gather.24.cloned.1.call-start = ((), (), s32[]{:S(2)}) async-start(), calls=%async_computation.24 | async-start | bytes 5474304 | tf_op jit(solution)/shard_map/all_gather | solution.py:230
  12.3 264.9 %all-gather.22.cloned.1.call-start = ((), (), s32[]{:S(2)}) async-start(), calls=%async_computation.23 | async-start | bytes 5474304 | tf_op jit(solution)/shard_map/all_gather | solution.py:229
  14.0 331.1 %all-gather.26.cloned.1.call-start = ((), (), s32[]{:S(2)}) async-start(), calls=%async_computation.25 | async-start | bytes 5474304 | tf_op jit(solution)/shard_map/all_gather | solution.py:228
  15.8 397.3 %all-gather.28.cloned.1.call-start = ((), (), s32[]{:S(2)}) async-start(), calls=%async_computation.26 | async-start | bytes 5474304 | tf_op jit(solution)/shard_map/all_gather | solution.py:233
  17.5 484.7 %all-gather.18.cloned.1.call-start = ((), (), s32[]{:S(2)}) async-start(), calls=%async_computation.11 | async-start | bytes 10948608 | tf_op jit(solution)/shard_map/all_gather | solution.py:234
  18.1 572.8 %all-gather.20.cloned.1.call-start = ((), (), s32[]{:S(2)}) async-start(), calls=%async_computation.12 | async-start | bytes 10948608 | tf_op jit(solution)/shard_map/all_gather | solution.py:235
  18.8 684.5 %all-gather.16.cloned.1.call-start = ((), (), s32[]{:S(2)}) async-start(), calls=%async_computation.10 | async-start | bytes 16422912 | tf_op jit(solution)/shard_map/all_gather | solution.py:226
  19.6 2216.7 %reduce-scatter.27.cloned.1.call-start = ((), (), s32[]{:S(2)}) async-start(), calls=%async_computation.21 | async-start | bytes 15925248 | tf_op jit(solution)/shard_map/reduce_scatter | solution.py:332
  142.4 1154.3 %copy-start.81 = (f32[1152]{0:T(1024)}, f32[1152]{0:T(1024)S(1)}, u32[]{:S(2)}) copy-start(f32[1152]{0:T(1024)S(1)} %get-tuple-element.1824) | copy-start | bytes 13828
  611.3 121.1 %copy-start.105 = (bf16[1,1152]{1,0:T(2,128)(2,1)S(1)}, bf16[1,1152]{1,0:T(2,128)(2,1)}, u32[]{:S(2)}) copy-start(bf16[1,1152]{1,0:T(2,128)(2,1)} %param.35) | copy-start | bytes 6916
  743.6 618.8 %copy-start.71 = (f32[1152]{0:T(1024)}, f32[1152]{0:T(1024)S(1)}, u32[]{:S(2)}) copy-start(f32[1152]{0:T(1024)S(1)} %get-tuple-element.1622) | copy-start | bytes 13828
  802.3 493.3 %collective-permute-start.1 = (bf16[1,1,32,1152]{3,2,1,0:T(8,128)(2,1)}, bf16[1,1,32,1152]{3,2,1,0:T(8,128)(2,1)S(1)}, u32[]{:S(2)}, u32[]{:S(2)}) collective-permute-start(bf16[1,1,32,1152]{3,2,1,0:T(8,128)(2,1)} %get-tuple-element.1823), channel_id=1, source_target_pairs={{1,0},{3,2},{5,4},{7,6},{9,8},{11,10},{13,12},{15,14},{17,16},{19,... | collective-permute-start | bytes 221192 | tf_op jit(solution)/shard_map/ppermute | solution.py:47
  803.6 492.1 %collective-permute-start = (bf16[1,1,32,1152]{3,2,1,0:T(8,128)(2,1)}, bf16[1,1,32,1152]{3,2,1,0:T(8,128)(2,1)S(1)}, u32[]{:S(2)}, u32[]{:S(2)}) collective-permute-start(bf16[1,1,32,1152]{3,2,1,0:T(8,128)(2,1)} %get-tuple-element.1822), channel_id=1, source_target_pairs={{0,1},{2,3},{4,5},{6,7},{8,9},{10,11},{12,13},{14,15},{16,17},{18,... | collective-permute-start | bytes 221192 | tf_op jit(solution)/shard_map/ppermute | solution.py:44
  1197.1 92.3 %copy-start.58 = (f32[512,16]{0,1:T(8,128)}, f32[512,16]{0,1:T(8,128)S(1)}, u32[]{:S(2)}) copy-start(f32[512,16]{0,1:T(8,128)S(1)} %copy.636) | copy-start | bytes 98308
  1208.9 80.5 %copy-start.7 = (f32[1,16,72,72]{3,2,1,0:T(8,128)}, f32[1,16,72,72]{3,2,1,0:T(8,128)S(1)}, u32[]{:S(2)}) copy-start(f32[1,16,72,72]{3,2,1,0:T(8,128)S(1)} %get-tuple-element.959) | copy-start | bytes 995332
  1318.5 42.4 %copy-start.26 = (f32[1,512,1152]{2,1,0:T(8,128)}, f32[1,512,1152]{2,1,0:T(8,128)S(1)}, u32[]{:S(2)}) copy-start(f32[1,512,1152]{2,1,0:T(8,128)S(1)} %get-tuple-element.1787) | copy-start | bytes 7077892
  1318.6 42.4 %copy-start.107 = (f32[512]{0:T(512)}, f32[512]{0:T(512)S(1)}, u32[]{:S(2)}) copy-start(f32[512]{0:T(512)S(1)} %broadcast_multiply_fusion) | copy-start | bytes 6148
  1377.1 71.9 %copy-start.2 = (f32[1,512,16,72]{1,3,2,0:T(8,128)}, f32[1,512,16,72]{1,3,2,0:T(8,128)S(1)}, u32[]{:S(2)}) copy-start(f32[1,512,16,72]{1,3,2,0:T(8,128)S(1)} %get-tuple-element.1783) | copy-start | bytes 7077892
  1491.7 755.3 %reduce-scatter.29.cloned.1.call-start = ((), (), s32[]{:S(2)}) async-start(), calls=%async_computation.22 | async-start | bytes 15925248 | tf_op jit(solution)/shard_map/reduce_scatter | solution.py:338
  1689.7 607.5 %reduce-scatter.23.cloned.1.call-start = ((), (), s32[]{:S(2)}) async-start(), calls=%async_computation.19 | async-start | bytes 36864 | tf_op jit(solution)/shard_map/reduce_scatter | solution.py:468
  1976.3 117.3 %collective-permute-start.3 = (bf16[1,1,32,1152]{3,2,1,0:T(8,128)(2,1)}, bf16[1,1,32,1152]{3,2,1,0:T(8,128)(2,1)}, u32[]{:S(2)}, u32[]{:S(2)}) collective-permute-start(bf16[1,1,32,1152]{3,2,1,0:T(8,128)(2,1)} %get-tuple-element.1821), channel_id=1, source_target_pairs={{1,0},{3,2},{5,4},{7,6},{9,8},{11,10},{13,12},{15,14},{17,16},{19,... | collective-permute-start | bytes 221192 | tf_op jit(solution)/shard_map/ppermute | solution.py:47
  1977.6 116.1 %collective-permute-start.2 = (bf16[1,1,32,1152]{3,2,1,0:T(8,128)(2,1)}, bf16[1,1,32,1152]{3,2,1,0:T(8,128)(2,1)}, u32[]{:S(2)}, u32[]{:S(2)}) collective-permute-start(bf16[1,1,32,1152]{3,2,1,0:T(8,128)(2,1)} %get-tuple-element.1820), channel_id=1, source_target_pairs={{0,1},{2,3},{4,5},{6,7},{8,9},{10,11},{12,13},{14,15},{16,17},{18,... | collective-permute-start | bytes 221192 | tf_op jit(solution)/shard_map/ppermute | solution.py:44
  2035.4 262.6 %reduce-scatter.21.cloned.1.call-start = ((), (), s32[]{:S(2)}) async-start(), calls=%async_computation.18 | async-start | bytes 61440 | tf_op jit(solution)/shard_map/reduce_scatter | solution.py:462
  2093.6 205.2 %reduce-scatter.13.cloned.1.call-start = ((), (), s32[]{:S(2)}) async-start(), calls=%async_computation.14 | async-start | bytes 24576 | tf_op jit(solution)/shard_map/reduce_scatter | solution.py:441
  2138.8 225.8 %reduce-scatter.15.cloned.1.call-start = ((), (), s32[]{:S(2)}) async-start(), calls=%async_computation.15 | async-start | bytes 3981312 | tf_op jit(solution)/shard_map/reduce_scatter | solution.py:444
  2153.7 215.9 %reduce-scatter.17.cloned.1.call-start = ((), (), s32[]{:S(2)}) async-start(), calls=%async_computation.16 | async-start | bytes 3981312 | tf_op jit(solution)/shard_map/reduce_scatter | solution.py:450
  2168.4 206.1 %reduce-scatter.25.cloned.1.call-start = ((), (), s32[]{:S(2)}) async-start(), calls=%async_computation.20 | async-start | bytes 3981312 | tf_op jit(solution)/shard_map/reduce_scatter | solution.py:474
  2185.0 194.5 %reduce-scatter.19.cloned.1.call-start = ((), (), s32[]{:S(2)}) async-start(), calls=%async_computation.17 | async-start | bytes 3981312 | tf_op jit(solution)/shard_map/reduce_scatter | solution.py:456
  2196.7 296.7 %reduce-scatter.11.cloned.1.call-start = ((), (), s32[]{:S(2)}) async-start(), calls=%async_computation.13 | async-start | bytes 23887872 | tf_op jit(solution)/shard_map/reduce_scatter | solution.py:435
  2236.2 628.0 %all-reduce.33.cloned.1.call-start = ((), (), s32[]{:S(2)}) async-start(), calls=%async_computation.29 | async-start | bytes 42467328
  2257.7 1073.5 %all-reduce.31.cloned.1.call-start = ((), (), s32[]{:S(2)}) async-start(), calls=%async_computation.28 | async-start | bytes 53084160
  (160 other events, 862.8 us)
Sparse Core Ops, SparseCore 0:
  15.2 122.7 all-reduce.28
  141.5 67.5 all-gather.23
  212.7 64.5 all-gather.21
  280.6 64.5 all-gather.25
  348.5 64.5 all-gather.27
  415.9 86.2 all-gather.17
  505.1 85.7 all-gather.19
  593.9 109.4 all-gather.15
  1491.8 121.4 reduce-scatter.26
  1689.8 120.9 reduce-scatter.28
  2035.5 7.5 reduce-scatter.22
  2093.7 7.6 reduce-scatter.20
  2138.9 7.5 reduce-scatter.12
  2153.8 35.6 reduce-scatter.14
  2191.7 37.9 reduce-scatter.16
  2231.8 38.4 reduce-scatter.24
  2272.4 38.7 reduce-scatter.18
  2313.3 179.9 reduce-scatter.10
  2498.0 366.1 all-reduce.32
  2870.1 461.0 all-reduce.30
where the time goes:
time: 3390 us; the launch traced here: 3350 us
  waiting for transfers between devices  1350 us (40%)
  local copies, waits for them, and re-layouts  926 us (27%)
  matrix products  586 us (17%)
  other arithmetic  318 us (9%)
  blocking collectives  138 us (4%)
    unnamed x23, waiting for transfers between devices  936 us
    rev x9, local copies, waits for them, and re-layouts, reverse_rows(): return jnp.flip(tensor, axis=1)  251 us
    dot_general x64, matrix products, advance(): jnp.einsum('she,shf->hef', k_part * remaining[:, :, None], v_part, precis...  130 us
    dot_general x64, matrix products, advance(): jnp.einsum('the,she->tsh', q_part, k_part, precision=highest) * weight  110 us
    reduce_scatter x1, waiting for transfers between devices, on_device(): lax.psum_scatter(sectioned(grad_ada.reshape(-1)).astype(jnp.bfloat16), 's...  109 us
    dot_general x64, matrix products, advance(): jnp.einsum('the,hef->thf', q_part, carried, precision=highest)  97.6 us
    all_gather x1, waiting for transfers between devices, on_device(): lax.all_gather(shards[0], ('dp', 'seq'), axis=0, tiled=True)  92 us
    dot_general x48, matrix products, advance(): within = jnp.einsum('tsh,shf->thf', scores, v_part, precision=highest)  79.8 us
  transfers between devices with their start and end apart: 24, of which 11 were waited for; matrix products, arithmetic and copies ran while one was open for 46% of the time, Pallas kernels for 0%

commit v1 on v0

v1 whole, which is shorter than its diff:
```python
import functools

import jax
import jax.numpy as jnp
import numpy as np
from jax import lax
from jax.experimental import pallas as pl
from jax.experimental.pallas import tpu as pltpu
from jax.sharding import PartitionSpec as P

GRID = 32
LANES = 128
GROUPS = 32
epsilon = 1e-06
f32 = jnp.float32
bf16 = jnp.bfloat16
VMEM_LIMIT = 56 * 1024 * 1024
FORWARD_PLAN = (
    ("f", 0, 0, 0), ("g", 0, 0, 0), -1, ("f", 1, 0, 0), ("f", 0, 0, 1), ("f", 2, 0, 0), ("g", 2, 0, 0),
    ("g", 1, 0, 0), ("f", 1, 0, 1), ("f", 5, 0, 0), ("f", 2, 0, 1), ("f", 0, 0, 2), ("g", 3, 0, 0), ("f", 0, 0, 3),
    ("f", 1, 0, 2), ("g", 0, 0, 1), ("f", 5, 0, 1), ("f", 2, 0, 2), ("f", 2, 0, 3), ("f", 1, 0, 3), ("g", 4, 0, 0),
    ("g", 5, 0, 0), ("g", 2, 0, 1), ("g", 1, 0, 1), ("f", 5, 0, 2), ("f", 5, 0, 3), ("g", 0, 0, 2), -1,
    ("g", 4, 0, 1), ("g", 5, 0, 1), ("g", 2, 0, 2), ("s", 0, 0, 0), ("s", 0, 0, 1), ("s", 0, 0, 2), ("s", 0, 0, 3),
    ("s", 1, 0, 0), ("g", 1, 0, 2), ("s", 1, 0, 1), -1, ("s", 1, 0, 2), ("s", 1, 0, 3), ("s", 2, 0, 0),
    ("g", 4, 0, 2), ("s", 2, 0, 1), ("s", 2, 0, 2), ("s", 2, 0, 3), ("g", 5, 0, 2), ("s", 3, 0, 0), ("g", 0, 0, 3),
    ("g", 4, 0, 3), ("g", 0, 1, 0), ("s", 3, 0, 1), ("g", 2, 0, 3), ("g", 1, 0, 3), ("g", 2, 1, 0), ("s", 3, 0, 2),
    ("g", 1, 1, 0), ("s", 3, 0, 3), ("g", 5, 0, 3), ("g", 3, 1, 0), ("g", 0, 1, 1), -1, ("g", 4, 1, 0),
    ("g", 5, 1, 0), ("g", 0, 1, 2), ("g", 2, 1, 1), ("g", 1, 1, 1), -1, ("g", 2, 1, 2), ("g", 1, 1, 2), -1,
    ("g", 4, 1, 1), -1, ("g", 5, 1, 1), -1, ("g", 0, 1, 3), -1, -1, ("g", 4, 1, 2), ("g", 5, 1, 2), ("g", 1, 1, 3),
    -1, -1, -1, ("g", 2, 1, 3), ("g", 4, 1, 3), -1, -1, -1, ("g", 5, 1, 3),
)
FEED_PLAN = (
    ("g", 0, 0, 0), -1, -1, ("g", 2, 0, 0), ("g", 1, 0, 0), ("g", 3, 0, 0), ("g", 0, 0, 1), -1, -1, ("g", 0, 0, 2),
    ("g", 4, 0, 0), ("g", 5, 0, 0), ("d", 0, 0, 0), ("g", 2, 0, 1), ("d", 4, 0, 0), -1, ("g", 1, 0, 1),
    ("g", 2, 0, 2), -1, ("g", 0, 0, 3), ("g", 1, 0, 2), ("d", 1, 0, 0), ("d", 2, 0, 0), ("d", 0, 0, 1),
    ("g", 4, 0, 1), -1, -1, ("g", 5, 0, 1), ("g", 2, 0, 3), ("d", 4, 0, 1), ("d", 0, 0, 2), -1, ("g", 1, 0, 3),
    ("g", 4, 0, 2), ("g", 5, 0, 2), ("d", 3, 0, 0), -1, -1, ("d", 4, 0, 2), ("d", 0, 0, 3), ("d", 2, 0, 1),
    ("d", 1, 0, 1), -1, -1, ("g", 4, 0, 3), -1, ("d", 1, 0, 2), ("d", 2, 0, 2), -1, -1, ("g", 5, 0, 3),
    ("d", 2, 0, 3), -1, ("d", 4, 0, 3), ("d", 1, 0, 3), ("d", 3, 0, 1), ("d", 5, 0, 0), -1, -1, -1, -1,
    ("d", 3, 0, 2), -1, -1, -1, -1, ("d", 3, 0, 3), ("d", 5, 0, 1), -1,
)
BACKWARD_PLAN = (
    -1, ("u", 0, 0, 0), ("u", 4, 0, 0), -1, ("u", 0, 0, 1), ("u", 0, 0, 2), ("u", 2, 0, 0), ("u", 1, 0, 0),
    ("u", 4, 0, 1), -1, ("u", 0, 0, 3), ("u", 2, 0, 1), ("u", 1, 0, 1), -1, ("u", 4, 0, 2), ("u", 2, 0, 2),
    ("u", 1, 0, 2), ("u", 3, 0, 0), -1, ("u", 2, 0, 3), ("u", 1, 0, 3), -1, ("u", 4, 0, 3), -1, ("u", 3, 0, 1),
    ("u", 5, 0, 0), -1, -1, ("u", 3, 0, 2), -1, -1, ("u", 3, 0, 3), ("u", 5, 0, 1), -1, -1, -1, -1, -1, -1,
)
FINISH_PLAN = (
    -1, ("a", 0, 0, 0), ("a", 4, 0, 0), -1, -1, ("a", 0, 0, 1), -1, ("g", 0, 0, 0), ("a", 2, 0, 0), ("a", 1, 0, 0),
    ("a", 4, 0, 1), ("s", 0, 0, 0), ("g", 1, 0, 0), ("g", 2, 0, 0), ("g", 0, 0, 1), ("s", 0, 0, 1), ("a", 0, 0, 2),
    ("s", 0, 0, 2), ("s", 0, 0, 3), ("g", 2, 0, 1), ("g", 5, 0, 0), ("g", 1, 0, 1), ("s", 1, 0, 0), ("a", 3, 0, 0),
    ("s", 2, 0, 0), ("s", 1, 0, 1), ("s", 2, 0, 1), ("g", 0, 0, 2), ("a", 1, 0, 1), ("a", 2, 0, 1), ("a", 4, 0, 2),
    ("s", 2, 0, 2), ("s", 2, 0, 3), ("a", 1, 0, 2), ("s", 1, 0, 2), ("g", 1, 0, 2), ("s", 1, 0, 3), ("g", 5, 0, 1),
    ("a", 2, 0, 2), ("g", 2, 0, 2), ("g", 0, 0, 3), ("s", 3, 0, 0), ("a", 0, 0, 3), ("a", 3, 0, 1), ("g", 2, 0, 3),
    ("g", 5, 0, 2), ("g", 1, 0, 3), ("s", 3, 0, 1), ("a", 4, 0, 3), ("a", 2, 0, 3), ("a", 1, 0, 3), ("a", 3, 0, 2),
    ("g", 5, 0, 3), ("s", 3, 0, 2), ("a", 5, 0, 0), ("a", 3, 0, 3), ("a", 5, 0, 1), ("s", 3, 0, 3),
)


def dot(a, b):
    return jnp.dot(a, b, preferred_element_type=f32)


def dot_bt(a, b):
    return lax.dot_general(a, b, (((1,), (1,)), ((), ())), preferred_element_type=f32)


def dot_at(a, b):
    return lax.dot_general(a, b, (((0,), (0,)), ((), ())), preferred_element_type=f32)


def halves(a):
    high = a.astype(bf16)
    return high, (a - high.astype(f32)).astype(bf16)


def spans(width, size=512):
    return [slice(start, min(start + size, width)) for start in range(0, width, size)]


def head_lanes(rows, width, start, head_width):
    head = lax.broadcasted_iota(jnp.int32, (rows, width), 0)
    lane = lax.broadcasted_iota(jnp.int32, (rows, width), 1) + start
    return (lane >= head * head_width) & (lane < (head + 1) * head_width)


def pick_left(rows, slot):
    out = lax.broadcasted_iota(jnp.int32, (4 * GROUPS, 16 * GROUPS), 0)
    src = lax.broadcasted_iota(jnp.int32, (4 * GROUPS, 16 * GROUPS), 1)
    return (src == (out // 4) * 16 + slot * 4 + out % 4).astype(bf16)


def norm_parts(values):
    center = jnp.mean(values, axis=-1, keepdims=True)
    centered = values - center
    spread = jnp.mean(centered * centered, axis=-1, keepdims=True)
    rstd = lax.rsqrt(spread + epsilon)
    return centered * rstd, rstd


def call(kernel, out_shape, name, **kw):
    return pl.pallas_call(
        kernel,
        out_shape=out_shape,
        name=name,
        compiler_params=pltpu.CompilerParams(vmem_limit_bytes=VMEM_LIMIT),
        **kw,
    )


def sds(shape, dtype=f32):
    return jax.ShapeDtypeStruct(shape, dtype)


def first_part(x_ref, mod_ref, perm_ref, wf_ref, bf_ref, xp_ref, gate_ref, run_ref, runt_ref):
    length = x_ref.shape[0]
    normed, _ = norm_parts(x_ref[...].astype(f32))
    hidden = (normed * (1.0 + mod_ref[1:2, :]) + mod_ref[0:1, :]).astype(bf16)
    for cols in spans(x_ref.shape[1]):
        xp_ref[:, cols] = dot(hidden, perm_ref[:, cols]).astype(bf16)

    gate = dot(xp_ref[...], wf_ref[...]) + bf_ref[...]
    gate_ref[...] = gate
    decay = -(jnp.maximum(gate, 0.0) + jnp.log1p(jnp.exp(-jnp.abs(gate))))
    row = lax.broadcasted_iota(jnp.int32, (length, length), 0)
    col = lax.broadcasted_iota(jnp.int32, (length, length), 1)
    tri = (row >= col).astype(bf16)
    high, rest = halves(decay)
    rest32 = decay - high.astype(f32)
    low = (rest32 - rest.astype(f32)).astype(bf16)
    inclusive = dot(tri, high) + dot(tri, rest) + dot(tri, low)
    exclusive = inclusive - decay
    run_ref[0] = inclusive
    run_ref[1] = exclusive
    runt_ref[0] = inclusive.T
    runt_ref[1] = exclusive.T


def project_part(slot, xp_ref, main_ref, left_ref, write):
    pick = pick_left(None, slot)
    main_rows = rows_in(main_ref)

    for cols in spans(xp_ref.shape[1]):
        main = main_ref[..., cols].reshape(main_rows, -1)
        left = dot(pick, left_ref[..., cols].reshape(16 * GROUPS, -1)).astype(bf16)
        write(cols, dot(xp_ref[:, :main_rows], main) + dot(xp_ref[:, main_rows:], left))


def two_terms(scale):
    return jnp.concatenate(halves(scale), axis=1)


def spread_heads(terms, cols, head_width):
    spread = head_lanes(LANES, cols.stop - cols.start, cols.start, head_width).astype(bf16)
    return dot(terms, jnp.concatenate([spread, spread], axis=0))


def head_sums(values, cols, head_width):
    return dot_bt(values, head_lanes(LANES, cols.stop - cols.start, cols.start, head_width).astype(bf16))


def own_block(shape, row_start, lane_start, head_width):
    row = lax.broadcasted_iota(jnp.int32, (shape[0], 1), 0) + row_start
    lane = lax.broadcasted_iota(jnp.int32, (1, shape[1]), 1) + lane_start
    same = None
    for head in range(
        max(row_start, lane_start) // head_width,
        min(row_start + shape[0] - 1, lane_start + shape[1] - 1) // head_width + 1,
    ):
        low, high = head * head_width, (head + 1) * head_width
        both = ((row >= low) & (row < high)) & ((lane >= low) & (lane < high))
        same = both if same is None else same | both
    if same is None:
        return jnp.broadcast_to(row < 0, shape)
    return same


def rows_in(ref):
    return int(np.prod(ref.shape[:-1]))


def near_lanes(cols, width, head_width):
    low = cols.start // head_width * head_width // LANES * LANES
    last = (cols.stop - 1) // head_width
    return slice(low, min(width, -(-(last + 1) * head_width // LANES) * LANES))


def unfolded(ref, way, near, cols, head_width):
    folded = ref[way, near, :]
    return jnp.concatenate([
        jnp.where(own_block(folded.shape, near.start, at, head_width), folded, 0)
        for at in range(cols.start, cols.stop, LANES)
    ], axis=1)


def state_part(head_width, ways, left, right_ref, scale_ref, out_ref):
    width = right_ref.shape[1]
    terms = [two_terms(scale_ref[way]) for way in range(ways)]
    for cols in spans(width, 2 * LANES):
        near = near_lanes(cols, width, head_width)
        mask = own_block((cols.stop - cols.start, near.stop - near.start), cols.start, near.start, head_width)
        for way in range(ways):
            scaled = left(cols).astype(f32) * spread_heads(terms[way], cols, head_width)
            product = jnp.where(mask, dot_at(scaled.astype(bf16), right_ref[:, near]), 0.0)
            total = product[:, :LANES]
            for at in range(LANES, near.stop - near.start, LANES):
                total = total + product[:, at : at + LANES]
            out_ref[way, cols, :] = total.astype(bf16)


def edge_part(source, out):
    for t in range(source.shape[1] // LANES):
        out(t, source[:, t * LANES : (t + 1) * LANES])


def pair_weights(run_ref, runt_ref, head, rows, length):
    count = rows.size
    own = lax.broadcasted_iota(jnp.int32, (count, LANES), 1) == head
    inc_t = jnp.sum(jnp.where(own, run_ref[0, rows, :], 0.0), axis=1, keepdims=True)
    exc_t = jnp.sum(jnp.where(own, run_ref[1, rows, :], 0.0), axis=1, keepdims=True)
    inc_s = runt_ref[0, pl.ds(head, 1), :]
    exc_s = runt_ref[1, pl.ds(head, 1), :]
    weight = jnp.exp(jnp.minimum(inc_t - inc_s, exc_s - exc_t))
    row = lax.broadcasted_iota(jnp.int32, (count, length), 0) + rows.start
    col = lax.broadcasted_iota(jnp.int32, (count, length), 1)
    return jnp.where(row == col, 2.0, weight)


def window_of(head, heads, head_width):
    start = pl.multiple_of(((head * head_width) // LANES - head // (heads - 1)) * LANES, LANES)
    return pl.ds(start, 2 * LANES), start


def own_lanes(rows, start, head, head_width):
    lane = lax.broadcasted_iota(jnp.int32, (rows, 2 * LANES), 1) + start
    return (lane >= head * head_width) & (lane < (head + 1) * head_width)


def row_blocks(length):
    size = min(length, 2 * LANES)
    return [pl.ds(start, size) for start in range(0, length, size)]


def mix_part(head_width, heads, low, high, qkv_ref, run_ref, runt_ref, mix_ref):
    length, width = mix_ref.shape

    @pl.loop(low // 2, high // 2)
    def _(pair):
        for odd in range(2):
            head = pair * 2 + odd
            win, start = window_of(head, heads, head_width)
            mask = own_lanes(length, start, head, head_width)
            keys = jnp.where(mask, qkv_ref[1, :, win], 0)
            vals = jnp.where(mask, qkv_ref[2, :, win], 0)
            for rows in row_blocks(length):
                weight = pair_weights(run_ref, runt_ref, head, rows, length)
                score = dot_bt(qkv_ref[0, rows, win], keys)
                mix_ref[rows, win] += dot((score * weight).astype(bf16), vals)


def fill_padded(pad_ref, rims_ref, middle):
    length = pad_ref.shape[0] - 2 * GRID
    pad_ref[:GRID, :] = rims_ref[0]
    pad_ref[GRID : GRID + length, :] = middle
    pad_ref[GRID + length :, :] = rims_ref[1]


def mixed_part(head_width, ways, qkv_ref, taken_ref, state_ref, taps_ref, vpad, mix_ref, mixed):
    length, width = mix_ref.shape
    place = lax.broadcasted_iota(jnp.int32, (length, LANES), 0) % GRID
    sums = jnp.zeros((length, LANES), f32)
    terms = [two_terms(taken_ref[way]) for way in range(ways)]
    for cols in spans(width, 2 * LANES):
        gained = mix_ref[:, cols]
        near = near_lanes(cols, width, head_width)
        for way in range(ways):
            block = unfolded(state_ref, way, near, cols, head_width)
            gained = gained + spread_heads(terms[way], cols, head_width) * dot(qkv_ref[0, :, near], block)
        mix_ref[:, cols] = gained
        sums = sums + head_sums((gained * gained).astype(bf16), cols, head_width)
    inverse = two_terms(lax.rsqrt(sums * (1.0 / head_width) + epsilon))
    for span in spans(width, 2 * LANES):
        normed = mix_ref[:, span] * spread_heads(inverse, span, head_width)
        for start in range(span.start, span.stop, LANES):
            cols = slice(start, start + LANES)
            conv = jnp.zeros((length, LANES), f32)
            for lateral in range(3):
                column = jnp.zeros((length, LANES), f32)
                for vertical in range(3):
                    tap = taps_ref[3 * vertical + lateral : 3 * vertical + lateral + 1, cols]
                    column = column + tap * vpad[vertical * GRID : vertical * GRID + length, cols].astype(f32)
                if lateral == 0:
                    column = jnp.where(place > 0, pltpu.roll(column, 1, 0), 0.0)
                if lateral == 2:
                    column = jnp.where(place < GRID - 1, pltpu.roll(column, length - 1, 0), 0.0)
                conv = conv + column
            own = normed[:, start - span.start : start - span.start + LANES]
            mixed[:, cols] = (own + (conv + taps_ref[9:10, cols])).astype(bf16)


def permute_part(source, perm_ref, out_ref):
    for cols in spans(perm_ref.shape[1]):
        out_ref[:, cols] = dot(source[...], perm_ref[:, cols]).astype(bf16)


def branch_part(x_ref, mod_ref, mixedp_ref, main_ref, left_ref, branch_ref, middle_ref):
    def write(cols, branch):
        branch_ref[:, cols] = branch.astype(bf16)
        middle_ref[:, cols] = x_ref[:, cols].astype(f32) + mod_ref[2:3, cols] * branch

    project_part(3, mixedp_ref, main_ref, left_ref, write)


def second_hidden(mod_ref, middle_ref, mixed):
    normed, _ = norm_parts(middle_ref[...])
    mixed[...] = (normed * (1.0 + mod_ref[4:5, :]) + mod_ref[3:4, :]).astype(bf16)


def project_kernel(xp_ref, main_ref, left_ref, out_ref):
    def write(cols, value):
        out_ref[0, :, cols] = value.astype(bf16)

    project_part(pl.program_id(0), xp_ref, main_ref, left_ref, write)


def state_kernel(head_width, ways, left_ref, right_ref, scale_ref, edge_ref, out_ref):
    width = right_ref.shape[1]
    state_part(head_width, ways, lambda cols: left_ref[:, cols], right_ref, scale_ref, out_ref)
    for way in range(ways):

        def write(t, value, way=way):
            out_ref[way, width + t * GRID : width + (t + 1) * GRID, :] = value

        edge_part(edge_ref[way], write)


def mix_kernel(head_width, heads, qkv_ref, run_ref, runt_ref, mix_ref):
    mix_ref[...] = jnp.zeros_like(mix_ref)
    mix_part(head_width, heads, 0, heads, qkv_ref, run_ref, runt_ref, mix_ref)


def after_kernel(
    head_width, ways, x_ref, mod_ref, perm_ref, qkv_ref, mix_in_ref, taken_ref, state_ref, rims_ref, taps_ref,
    main_ref, left_ref, mix_ref, mixedp_ref, branch_ref, middle_ref, h2p_ref, vpad, mixed,
):
    mix_ref[...] = mix_in_ref[...]
    fill_padded(vpad, rims_ref, qkv_ref[2])
    mixed_part(head_width, ways, qkv_ref, taken_ref, state_ref, taps_ref, vpad, mix_ref, mixed)
    permute_part(mixed, perm_ref, mixedp_ref)
    branch_part(x_ref, mod_ref, mixedp_ref, main_ref, left_ref, branch_ref, middle_ref)
    second_hidden(mod_ref, middle_ref, mixed)
    permute_part(mixed, perm_ref, h2p_ref)


def gelu_both(v):
    c = np.float32(np.sqrt(2.0 / np.pi))
    square = v * v
    th = jnp.tanh(c * (v + np.float32(0.044715) * (square * v)))
    half = 0.5 * (1.0 + th)
    slope = half + 0.5 * v * (1.0 - th * th) * (c * (1.0 + np.float32(3 * 0.044715) * square))
    return v * half, slope


def feed_kernel(
    h2p_ref, cot_ref, mod_ref, middle_ref, main_ref, left_ref, down_ref,
    out_ref, gh_ref, gup_ref, gleft_ref, gdown_ref, ggate_ref, down_acc, gdi, h2pt, act, actt, gup, left,
):
    j = pl.program_id(0)
    main_rows = main_ref.shape[0] * main_ref.shape[1]
    length, width = h2p_ref.shape

    @pl.when(j == 0)
    def _():
        gdi[...] = (cot_ref[...].astype(f32) * mod_ref[5:6, :]).astype(bf16)
        h2pt[...] = h2p_ref[...].T
        down_acc[...] = jnp.zeros_like(down_acc)
        gh_ref[...] = jnp.zeros_like(gh_ref)
        gleft_ref[...] = jnp.zeros_like(gleft_ref)

    pick = pick_left(None, j)
    left[...] = dot(pick, left_ref[...].reshape(16 * GROUPS, width)).astype(bf16)
    for cols in spans(width):
        main = main_ref[:, :, cols].reshape(main_rows, -1)
        up = dot(h2p_ref[:, :main_rows], main) + dot(h2p_ref[:, main_rows:], left[:, cols])
        value, slope = gelu_both(up)
        value = value.astype(bf16)
        act[:, cols] = value
        actt[cols, :] = value.T
        gup[:, cols] = (dot_bt(gdi[...], down_ref[cols, :]) * slope).astype(bf16)
    for cols in spans(width):
        down_acc[:, cols] += dot(act[...], down_ref[:, cols])
        gdown_ref[:, cols] = dot(actt[...], gdi[:, cols]).astype(bf16)
        gup_ref[:, :, cols] = dot(h2pt[:main_rows, :], gup[:, cols]).astype(bf16).reshape(GROUPS, 32, -1)
        part = dot(h2pt[main_rows:, :], gup[:, cols]).astype(bf16)
        gleft_ref[:, :, cols] += dot_at(pick, part).astype(bf16).reshape(GROUPS, 16, -1)
    gh_ref[:, main_rows:] += dot_bt(gup[...], left[...])
    for cols in spans(main_rows):
        gh_ref[:, cols] += dot_bt(gup[...], main_ref[cols.start // 32 : cols.stop // 32].reshape(-1, width))

    @pl.when(j == pl.num_programs(0) - 1)
    def _():
        out_ref[...] = (middle_ref[...] + mod_ref[5:6, :] * down_acc[...]).astype(bf16)
        ggate_ref[...] = jnp.sum(cot_ref[...].astype(f32) * down_acc[...], axis=0, keepdims=True)


def unpermute(perm_ref, source_ref, out_ref):
    source = source_ref[...].astype(bf16)
    for cols in spans(perm_ref.shape[0]):
        out_ref[:, cols] = dot_bt(source, perm_ref[cols, :])


def norm_back(normed, rstd, factor, grad):
    scaled = grad * (1.0 + factor)
    mean = jnp.mean(scaled, axis=-1, keepdims=True)
    along = jnp.mean(scaled * normed, axis=-1, keepdims=True)
    return (scaled - mean - normed * along) * rstd


def second_part(
    head_width, ghp_ref, perm_ref, middle_ref, mod_ref, cot_ref, branch_ref, mixedp_ref, mix_ref, main_ref, left_ref,
    gmid_ref, gmixed_ref, gmix_ref, gout_ref, gleft_ref, sums_ref, gh, gb, turned,
):
    length, width = middle_ref.shape
    main_rows = rows_in(main_ref)
    unpermute(perm_ref, ghp_ref, gh)
    yield
    normed, rstd = norm_parts(middle_ref[...])
    grad = gh[...]
    sums_ref[0:1, :] = jnp.sum(grad, axis=0, keepdims=True)
    sums_ref[1:2, :] = jnp.sum(grad * normed, axis=0, keepdims=True)
    grad_middle = cot_ref[...].astype(f32) + norm_back(normed, rstd, mod_ref[4:5, :], grad)
    gmid_ref[...] = grad_middle
    sums_ref[2:3, :] = jnp.sum(grad_middle * branch_ref[...].astype(f32), axis=0, keepdims=True)
    sums_ref[3:8, :] = jnp.zeros((5, width), f32)
    gb[...] = (grad_middle * mod_ref[2:3, :]).astype(bf16)
    pick = pick_left(None, 3)
    turned[...] = mixedp_ref[...].T
    yield
    for cols in spans(width):
        gout_ref[..., cols] = dot(turned[:main_rows, :], gb[:, cols]).astype(bf16).reshape(gout_ref.shape[:-1] + (-1,))
        part = dot(turned[main_rows:, :], gb[:, cols]).astype(bf16)
        gleft_ref[..., cols] = dot_at(pick, part).astype(bf16).reshape(gleft_ref.shape[:-1] + (-1,))
    left = dot(pick, left_ref[...].reshape(16 * GROUPS, width)).astype(bf16)
    gh[:, main_rows:] = dot_bt(gb[...], left)
    for cols in spans(main_rows):
        gh[:, cols] = dot_bt(gb[...], main_ref[cols.start // 32 : cols.stop // 32].reshape(-1, width))
    gb[...] = gh[...].astype(bf16)
    yield
    for cols in spans(width):
        gmixed_ref[:, cols] = dot_bt(gb[...], perm_ref[cols, :]).astype(bf16)

    sums = jnp.zeros((length, LANES), f32)
    dots = jnp.zeros((length, LANES), f32)
    for cols in spans(width, 2 * LANES):
        mix = mix_ref[:, cols]
        sums = sums + head_sums((mix * mix).astype(bf16), cols, head_width)
        for term in halves(mix * gmixed_ref[:, cols].astype(f32)):
            dots = dots + head_sums(term, cols, head_width)
    inverse = lax.rsqrt(sums * (1.0 / head_width) + epsilon)
    along = two_terms(dots * (1.0 / head_width) * inverse * inverse * inverse)
    inverse = two_terms(inverse)
    for cols in spans(width, 2 * LANES):
        gmix_ref[:, cols] = (
            gmixed_ref[:, cols].astype(f32) * spread_heads(inverse, cols, head_width)
            - mix_ref[:, cols] * spread_heads(along, cols, head_width)
        ).astype(bf16)
    yield


def second_kernel(head_width, *refs):
    for _ in second_part(head_width, *refs):
        pass


def pairs_part(head_width, heads, low, high, qkv_ref, gmix_ref, run_ref, runt_ref, gq_ref, gk_ref, gv_ref, rows_ref, cols_ref, held):
    length, width = gmix_ref.shape

    @pl.loop(low, high)
    def _(head):
        win, start = window_of(head, heads, head_width)
        mask = own_lanes(length, start, head, head_width)
        queries = jnp.where(mask, qkv_ref[0, :, win], 0)
        keys = jnp.where(mask, qkv_ref[1, :, win], 0)
        vals = jnp.where(mask, qkv_ref[2, :, win], 0)
        grads = jnp.where(mask, gmix_ref[:, win], 0)
        own = lax.broadcasted_iota(jnp.int32, (LANES, LANES), 1) == head
        row = lax.broadcasted_iota(jnp.int32, (LANES, LANES), 0)
        col = lax.broadcasted_iota(jnp.int32, (LANES, LANES), 1)
        columns = [None, None]
        for rows in row_blocks(length):
            weight = pair_weights(run_ref, runt_ref, head, rows, length)
            at = slice(rows.start, rows.start + rows.size)
            score = dot_bt(queries[at], keys) * weight
            grad = dot_bt(grads[at], vals)
            both = score * grad
            held[0, rows, :] = score.astype(bf16)
            held[1, rows, :] = (grad * weight).astype(bf16)
            for step in range(rows.size // LANES):
                first = rows.start + step * LANES
                strip = both[step * LANES : (step + 1) * LANES]
                middle = strip[:, first : first + LANES]
                pieces = [
                    (0, strip[:, :first], jnp.where(row > col, middle, 0.0)),
                    (1, strip[:, first + LANES :], jnp.where(row < col, middle, 0.0)),
                ]
                for way, part, corner in pieces:
                    total = jnp.sum(corner, axis=1, keepdims=True)
                    lines = [jnp.sum(corner, axis=0, keepdims=True)]
                    if first if way == 0 else length - first - LANES:
                        total = total + jnp.sum(part, axis=1, keepdims=True)
                        lines.insert(0 if way == 0 else 1, jnp.sum(part, axis=0, keepdims=True))
                    blank = jnp.zeros((1, length - sum(line.shape[1] for line in lines)), f32)
                    if blank.shape[1]:
                        lines.insert(len(lines) if way == 0 else 0, blank)
                    line = jnp.concatenate(lines, axis=1)
                    columns[way] = line if columns[way] is None else columns[way] + line
                    rows_ref[way, first : first + LANES, :] += jnp.where(own, total, 0.0)
        for way in range(2):
            cols_ref[way, pl.ds(head, 1), :] = columns[way]
        gq_ref[:, win] += dot(held[1], keys)
        gk_ref[:, win] += dot_at(held[1], queries)
        gv_ref[:, win] += dot_at(held[0], grads)


def pairs_kernel(head_width, heads, qkv_ref, gmix_ref, run_ref, runt_ref, gq_ref, gk_ref, gv_ref, rows_ref, cols_ref, held):
    for ref in (gq_ref, gk_ref, gv_ref, rows_ref, cols_ref):
        ref[...] = jnp.zeros_like(ref)
    pairs_part(
        head_width, heads, 0, heads, qkv_ref, gmix_ref, run_ref, runt_ref, gq_ref, gk_ref, gv_ref, rows_ref, cols_ref, held
    )


def carry_part(
    head_width, ways, early, qkv_ref, gmix_ref, gq_in, gk_in, gv_in, rows_ref, cols_ref, taken_ref, given_ref, gate_ref,
    state_ref, leave_ref, through, vpad, gpad, taps_ref, gqkv_ref, ggate_ref, conv_ref, bias_ref,
):
    length, width = gmix_ref.shape
    place = lax.broadcasted_iota(jnp.int32, (length, LANES), 0) % GRID
    taken_sums = [jnp.zeros((length, LANES), f32) for _ in range(ways)]
    given_sums = [jnp.zeros((length, LANES), f32) for _ in range(ways)]
    take_terms = [two_terms(taken_ref[way]) for way in range(ways)]
    give_terms = [two_terms(given_ref[way]) for way in range(ways)]
    for span in spans(width, 2 * LANES):
        near = near_lanes(span, width, head_width)
        gq, gk, gv = gq_in[:, span], gk_in[:, span], gv_in[:, span]
        for way in range(ways):
            take = spread_heads(take_terms[way], span, head_width)
            give = spread_heads(give_terms[way], span, head_width)
            back_q = take * dot_bt(gmix_ref[:, near], unfolded(state_ref, way, span, near, head_width))
            gq = gq + back_q
            for term in halves(qkv_ref[0, :, span].astype(f32) * back_q):
                taken_sums[way] = taken_sums[way] + head_sums(term, span, head_width)
            back_k = give * dot_bt(qkv_ref[2, :, near], unfolded(leave_ref, way, span, near, head_width))
            gk = gk + back_k
            for term in halves(qkv_ref[1, :, span].astype(f32) * back_k):
                given_sums[way] = given_sums[way] + head_sums(term, span, head_width)
            gv = gv + give * dot(qkv_ref[1, :, near], unfolded(leave_ref, way, near, span, head_width))
        gqkv_ref[0, :, span] = gq.astype(bf16)
        gqkv_ref[1, :, span] = gk.astype(bf16)
        for first in range(span.start, span.stop, LANES):
            cols = slice(first, first + LANES)
            grad = gpad[GRID : GRID + length, cols].astype(f32)
            total = gv[:, first - span.start : first - span.start + LANES]
            for lateral in range(3):
                b = lateral - 1
                column = jnp.zeros((length, LANES), f32)
                for vertical in range(3):
                    tap = taps_ref[3 * vertical + lateral : 3 * vertical + lateral + 1, cols]
                    start = (2 - vertical) * GRID
                    column = column + tap * gpad[start : start + length, cols].astype(f32)
                shifted = grad
                if b == -1:
                    column = jnp.where(place < GRID - 1, pltpu.roll(column, length - 1, 0), 0.0)
                    shifted = jnp.where(place < GRID - 1, pltpu.roll(grad, length - 1, 0), 0.0)
                if b == 1:
                    column = jnp.where(place > 0, pltpu.roll(column, 1, 0), 0.0)
                    shifted = jnp.where(place > 0, pltpu.roll(grad, 1, 0), 0.0)
                total = total + column
                for vertical in range(3):
                    window = vpad[vertical * GRID : vertical * GRID + length, cols].astype(f32)
                    conv_ref[3 * vertical + lateral : 3 * vertical + lateral + 1, cols] = jnp.sum(
                        window * shifted, axis=0, keepdims=True
                    )
            conv_ref[9:10, cols] = jnp.sum(grad, axis=0, keepdims=True)
            gqkv_ref[2, :, cols] = total.astype(bf16)
        if span.start // (2 * LANES) in (1, 3) or span.stop == width:
            yield
    conv_ref[10:16, :] = jnp.zeros((6, width), f32)

    row = lax.broadcasted_iota(jnp.int32, (length, length), 0)
    col = lax.broadcasted_iota(jnp.int32, (length, length), 1)
    before = (col < row).astype(bf16)
    upto = (col <= row).astype(bf16)

    def summed(product, matrix, value):
        high, rest = halves(value)
        low = (value - high.astype(f32) - rest.astype(f32)).astype(bf16)
        return product(matrix, high) + product(matrix, rest) + product(matrix, low)

    def columns(way):
        lines = cols_ref[way]
        if lines.shape[0] < LANES:
            lines = jnp.concatenate([lines, jnp.zeros((LANES - lines.shape[0], length), f32)], axis=0)
        return lines.T

    ahead = rows_ref[0] - columns(0)
    behind = rows_ref[1] - columns(1)
    if ways == 2:
        ahead, behind = ahead + taken_sums[0], behind + taken_sums[1]
        given_ahead, given_behind = given_sums
    else:
        ahead = ahead + taken_sums[0] * (1.0 - early)
        behind = behind + taken_sums[0] * early
        given_ahead, given_behind = given_sums[0] * early, given_sums[0] * (1.0 - early)
    grad_decay = (
        summed(dot_at, upto, ahead)
        + summed(dot, before, given_ahead)
        + summed(dot, upto, behind)
        + summed(dot_at, before, given_behind)
        + through
    )
    gate = gate_ref[...]
    small = jnp.exp(-jnp.abs(gate))
    sigmoid = jnp.where(gate >= 0, 1.0, small) / (1.0 + small)
    grad_gate = (-grad_decay * sigmoid).astype(bf16)
    lane = lax.broadcasted_iota(jnp.int32, grad_gate.shape, 1)
    grad_gate = jnp.where(lane < width // head_width, grad_gate.astype(f32), 0.0)
    ggate_ref[...] = grad_gate.astype(bf16)
    bias_ref[...] = jnp.sum(grad_gate, axis=0, keepdims=True)
    yield


def carry_kernel(
    head_width, ways, qkv_ref, gmix_ref, gq_in, gk_in, gv_in, rows_ref, cols_ref, taken_ref, given_ref, gate_ref,
    state_ref, leave_ref, through_ref, early_ref, gmixed_ref, grims_ref, vrims_ref, taps_ref,
    gqkv_ref, ggate_ref, conv_ref, bias_ref, vpad, gpad,
):
    fill_padded(vpad, vrims_ref, qkv_ref[2])
    fill_padded(gpad, grims_ref, gmixed_ref[...])
    for _ in carry_part(
        head_width, ways, early_ref[...], qkv_ref, gmix_ref, gq_in, gk_in, gv_in, rows_ref, cols_ref, taken_ref,
        given_ref, gate_ref, state_ref, leave_ref, through_ref[...], vpad, gpad, taps_ref, gqkv_ref, ggate_ref, conv_ref,
        bias_ref,
    ):
        pass


def projection_grads(slot, turned, grad_ref, gmain_ref, gleft_ref):
    pick = pick_left(None, slot)
    main_rows = rows_in(gmain_ref)
    for cols in spans(grad_ref.shape[1]):
        grad = grad_ref[:, cols]
        gmain_ref[..., cols] = dot(turned[:main_rows, :], grad).astype(bf16).reshape(gmain_ref.shape[:-1] + (-1,))
        part = dot(turned[main_rows:, :], grad).astype(bf16)
        gleft_ref[..., cols] += dot_at(pick, part).astype(bf16).reshape(gleft_ref.shape[:-1] + (-1,))


def projection_back(slot, grad_ref, main_ref, left_ref, gh_ref):
    width = grad_ref.shape[1]
    main_rows = rows_in(main_ref)
    left = dot(pick_left(None, slot), left_ref[...].reshape(16 * GROUPS, width)).astype(bf16)
    gh_ref[:, main_rows:] += dot_bt(grad_ref[...], left)
    for cols in spans(main_rows):
        gh_ref[:, cols] += dot_bt(grad_ref[...], main_ref[cols.start // 32 : cols.stop // 32].reshape(-1, width))


def weights_kernel(
    xp_ref, gqkv_ref, ggate_ref, wf_ref, main_ref, left_ref, gout_left_ref, gmain_ref, gleft_ref, gforget_ref, gh_ref, turned
):
    slot = pl.program_id(0)

    @pl.when(slot == 0)
    def _():
        turned[...] = xp_ref[...].T
        gleft_ref[...] = gout_left_ref[...]
        gh_ref[...] = dot_bt(ggate_ref[...], wf_ref[...])
        gforget_ref[...] = dot(turned[...], ggate_ref[...])

    projection_grads(slot, turned, gqkv_ref.at[0], gmain_ref, gleft_ref)
    projection_back(slot, gqkv_ref.at[0], main_ref, left_ref, gh_ref)


def last_part(ghp_ref, perm_ref, x_ref, mod_ref, gmid_ref, gin_ref, sums_ref, gh):
    unpermute(perm_ref, ghp_ref, gh)
    normed, rstd = norm_parts(x_ref[...].astype(f32))
    grad = gh[...]
    sums_ref[0:1, :] = jnp.sum(grad, axis=0, keepdims=True)
    sums_ref[1:2, :] = jnp.sum(grad * normed, axis=0, keepdims=True)
    gin_ref[...] = gmid_ref[...] + norm_back(normed, rstd, mod_ref[1:2, :], grad)


def ring_place(z):
    return z + (z // 2) * (5 - 2 * z)


class Here:
    def __init__(self):
        row, x = lax.axis_index("dp"), lax.axis_index("seq")
        z, y, core = row // 4, (row // 2) % 2, row % 2
        self.x, self.y, self.z, self.core = x, y, z, core
        self.p = ring_place(z)
        place = lambda z, y, core, x: ((z * 2 + y) * 2 + core, x)
        self.next = place(ring_place((self.p + 1) % 4), y, core, x)
        self.prev = place(ring_place((self.p + 3) % 4), y, core, x)
        self.over_y = place(z, 1 - y, core, x)
        self.over_x = place(z, y, core, 1 - x)
        self.sibling = place(z, y, 1 - core, x)

    def ring_z(self, back):
        return ring_place((self.p + 8 - back) % 4)

    def greet(self):
        barrier = pltpu.get_barrier_semaphore()
        for device in (self.next, self.prev, self.over_y, self.over_x, self.sibling):
            pl.semaphore_signal(barrier, inc=1, device_id=device, device_id_type=pl.DeviceIdType.MESH)
        pl.semaphore_wait(barrier, 5)


def push(source, target, send, recv, device):
    copy = pltpu.make_async_remote_copy(
        src_ref=source, dst_ref=target, send_sem=send, recv_sem=recv, device_id=device,
        device_id_type=pl.DeviceIdType.MESH,
    )
    copy.start()
    return copy


def routes(rows):
    tiles = rows // 16
    third = 2 if tiles >= 8 else 0
    first = -(-(tiles - third) // 2)
    cuts = [0, 16 * first, 16 * (tiles - third), rows]
    return [pl.ds(low, high - low) for low, high in zip(cuts, cuts[1:])]


class Gather:
    def __init__(self, tag, here, ins, outs, sems):
        self.here, self.ins, self.outs, self.sems = here, ins, outs, sems
        self.flights, self.todo, self.own = {}, {}, {}
        for i in range(len(ins)):
            a, b, c = routes(ins[i].shape[0])
            self.todo[tag, 0, i, 0] = (), functools.partial(self.along_z, i, 0)
            for s in range(4):
                if s:
                    self.todo[tag, 0, i, s] = (("z", i, s - 1),), functools.partial(self.along_z, i, s)
                self.todo[tag, 1, i, s] = (("a1", i, s),), functools.partial(self.second, i, s, 0)
                waits = [("a2", i, s)]
                if b.size:
                    self.todo[tag, 2, i, s] = (("b1", i, s),), functools.partial(self.second, i, s, 1)
                    waits.append(("b2", i, s))
                if c.size:
                    waits.append(("cy", i, 0) if s == 0 else ("cz", i, s - 1))
                    self.todo[tag, 4, i, s] = (waits[-1],), functools.partial(self.third, i, s)
                    waits[-1] = ("c", i, s)
                self.todo[tag, 5, i, s] = tuple(waits), functools.partial(self.across, i, s)
            if c.size:
                self.todo[tag, 3, i, 0] = (("cx", i, 0),), functools.partial(self.third_over_y, i)

    def send(self, key, number, source, target, device):
        i, s = key[1:]
        self.flights[key] = push(source, target, self.sems[0].at[number, i, s], self.sems[1].at[number, i, s], device)

    def start(self):
        here = self.here
        for i, block in enumerate(self.ins):
            target = self.outs[i].at[here.z, here.y, here.core, here.x]
            self.own[i] = pltpu.make_async_copy(block, target, self.sems[2].at[i])
            self.own[i].start()

    def run(self, name):
        waits, action = self.todo.pop(name)
        for key in waits:
            if key[0] != "c":
                self.flights[key].wait_recv()
        action()

    def settle(self, i):
        if i in self.own:
            self.own.pop(i).wait()

    def along_z(self, i, s):
        here = self.here
        a, b, c = routes(self.ins[i].shape[0])
        slot = self.outs[i].at[here.ring_z(s), here.y, here.core, here.x]
        held = self.ins[i] if s == 0 else slot
        if s < 3:
            both = pl.ds(0, a.size + b.size)
            self.send(("z", i, s), 0, held.at[both], slot.at[both], here.next)
        self.send(("a1", i, s), 1, held.at[a], slot.at[a], here.over_y)
        if b.size:
            self.send(("b1", i, s), 2, held.at[b], slot.at[b], here.over_x)
        if s == 0 and c.size:
            self.send(("cx", i, 0), 5, held.at[c], slot.at[c], here.over_x)

    def second(self, i, s, half):
        here, out = self.here, self.outs[i]
        a, b, c = routes(self.ins[i].shape[0])
        z = here.ring_z(s)
        if s == 0:
            self.settle(i)
        if half:
            block = out.at[z, here.y, here.core, :, b]
            self.send(("b2", i, s), 4, block, block, here.over_y)
        else:
            block = out.at[z, :, here.core, here.x, a]
            self.send(("a2", i, s), 3, block, block, here.over_x)

    def third_over_y(self, i):
        here = self.here
        c = routes(self.ins[i].shape[0])[2]
        self.settle(i)
        block = self.outs[i].at[here.z, here.y, here.core, :, c]
        self.send(("cy", i, 0), 6, block, block, here.over_y)

    def third(self, i, s):
        here = self.here
        c = routes(self.ins[i].shape[0])[2]
        if s < 3:
            block = self.outs[i].at[here.ring_z(s), :, here.core, :, c]
            self.send(("cz", i, s), 7, block, block, here.next)

    def across(self, i, s):
        here = self.here
        block = self.outs[i].at[here.ring_z(s), :, here.core]
        self.send(("core", i, s), 8, block, block, here.sibling)

    def arrived(self, i, places=range(4)):
        for s in places:
            self.flights["core", i, s].wait_recv()

    def finish(self):
        for copy in self.flights.values():
            copy.wait_send()


def gather_sems(count):
    dma = pltpu.SemaphoreType.DMA
    return [dma((9, count, 4)), dma((9, count, 4)), dma((count,))]


def gathered_shape(block):
    return sds((4, 2, 2, 2) + block.shape, block.dtype)


def add_rows(target, source, lead, low, size):
    chunk = 16

    @pl.loop(0, size // chunk)
    def _(r):
        start = pl.multiple_of(r * chunk, chunk)
        here, there = pl.ds(low + start, chunk), pl.ds(start, chunk)
        for at in lead:
            target[at + (here,)] = target[at + (here,)] + source[at + (there,)]


class Scatter:
    def __init__(self, tag, here, ins, final, scratch):
        (
            self.acc, self.mate, self.one_a, self.one_b, self.two_rows, self.ring_rows, self.ring_c, self.c_y, self.c_x,
            self.send_sem, self.recv_sem, self.load_sem,
        ) = scratch
        self.here, self.ins, self.final = here, ins, final
        self.rows = self.acc.shape[3]
        self.a, self.b, self.c = routes(self.rows)
        self.flights, self.loads, self.todo, self.released = {}, {}, {}, set()
        for k in range(4):
            self.todo[tag, 0, 0, k] = (("core", k),), functools.partial(self.from_sibling, k)
            self.todo[tag, 1, 0, k] = (("a1", k),), functools.partial(self.first_sum, k, 0)
            waits = [("a2", k)]
            if self.b.size:
                self.todo[tag, 2, 0, k] = (("b1", k),), functools.partial(self.first_sum, k, 1)
                waits.append(("b2", k))
            if k:
                waits.append(("z", k - 1))
            self.todo[tag, 3, 0, k] = tuple(waits), functools.partial(self.second_sum, k)
            if self.c.size:
                waits = (("c", k), ("cz", k - 1)) if k else (("c", k),)
                self.todo[tag, 4, 0, k] = waits, functools.partial(self.third_sum, k)
        if self.c.size:
            self.todo[tag, 5, 0, 0] = (("cy", 0),), self.third_over_y
            self.todo[tag, 5, 0, 1] = (("cx", 0), ("own", 0)), self.third_over_x

    def send(self, key, number, source, target, device, piece=0):
        at = (number + piece, key[1])
        self.flights[key] = push(source, target, self.send_sem.at[at], self.recv_sem.at[at], device)

    def pieces(self, k):
        z, low = self.here.ring_z(k + 1), 0
        for number, ref in enumerate(self.ins):
            if len(ref.shape) == 3:
                for y in range(2):
                    yield (
                        number + y, lambda core, y=y: ref.at[pl.ds(8 * z + 4 * y + 2 * core, 2)], lambda slot, y=y: slot.at[y]
                    )
            elif len(ref.shape) == 5:
                yield number, lambda core, ref=ref: ref.at[:, core], lambda slot: slot
            else:
                span = pl.ds(low, ref.shape[4])
                low += ref.shape[4]
                yield (
                    number, lambda core, ref=ref: ref.at[z, :, core], lambda slot, span=span: slot.at[:, :, span]
                )

    def load(self, k):
        for number, source, target in self.pieces(k):
            self.loads[k, number] = pltpu.make_async_copy(
                source(self.here.core), target(self.acc.at[k]), self.load_sem.at[k, number]
            )
            self.loads[k, number].start()

    def to_sibling(self, k):
        for number, source, target in self.pieces(k):
            self.send(
                ("core", k, number), 8, source(1 - self.here.core), target(self.mate.at[k]), self.here.sibling, number
            )

    def offer(self, k):
        self.load(k)
        self.to_sibling(k)

    def release(self, k):
        for number, _, _ in self.pieces(k):
            self.flights["core", k, number].wait_send()
        self.released.add(k)

    def prepare(self):
        for k in range(4):
            self.load(k)

    def start(self):
        for k in range(4):
            self.to_sibling(k)

    def run(self, name):
        waits, action = self.todo.pop(name)
        for key in waits:
            if key[0] == "core":
                for number, _, _ in self.pieces(key[1]):
                    self.loads[key[1], number].wait()
                    self.flights["core", key[1], number].wait_recv()
            elif key[0] not in ("c", "own"):
                self.flights[key].wait_recv()
        action()

    def from_sibling(self, k):
        here, acc = self.here, self.acc.at[k]
        add_rows(acc, self.mate.at[k], [(a, b) for a in range(2) for b in range(2)], 0, self.rows)
        self.send(("a1", k), 0, acc.at[:, 1 - here.x, self.a], self.one_a.at[k], here.over_x)
        if self.b.size:
            self.send(("b1", k), 1, acc.at[1 - here.y, :, self.b], self.one_b.at[k], here.over_y)

    def first_sum(self, k, half):
        here, acc = self.here, self.acc.at[k]
        if half:
            add_rows(acc.at[here.y], self.one_b.at[k], [(0,), (1,)], self.b.start, self.b.size)
            self.send(
                ("b2", k), 3, acc.at[here.y, 1 - here.x, self.b], self.two_rows.at[k, self.b], here.over_x
            )
        else:
            add_rows(acc.at[:, here.x], self.one_a.at[k], [(0,), (1,)], self.a.start, self.a.size)
            self.send(
                ("a2", k), 2, acc.at[1 - here.y, here.x, self.a], self.two_rows.at[k, self.a], here.over_y
            )

    def second_sum(self, k):
        here = self.here
        size = self.a.size + self.b.size
        mine = self.acc.at[k, here.y, here.x]
        add_rows(mine, self.two_rows.at[k], [()], 0, size)
        if k:
            add_rows(mine, self.ring_rows.at[k - 1], [()], 0, size)
        if k < 3:
            self.send(("z", k), 4, mine.at[pl.ds(0, size)], self.ring_rows.at[k], here.next)
        elif not self.c.size:
            self.final(mine)

    def third_sum(self, k):
        here, acc = self.here, self.acc.at[k]
        if k:
            add_rows(acc, self.ring_c.at[k - 1], [(a, b) for a in range(2) for b in range(2)], self.c.start, self.c.size)
        if k < 3:
            self.send(("cz", k), 5, acc.at[:, :, self.c], self.ring_c.at[k], here.next)
        else:
            self.send(("cy", 0), 6, acc.at[1 - here.y, :, self.c], self.c_y, here.over_y)

    def third_over_y(self):
        here, acc = self.here, self.acc.at[3]
        add_rows(acc.at[here.y], self.c_y, [(0,), (1,)], self.c.start, self.c.size)
        self.send(("cx", 0), 7, acc.at[here.y, 1 - here.x, self.c], self.c_x, here.over_x)

    def third_over_x(self):
        mine = self.acc.at[3, self.here.y, self.here.x]
        add_rows(mine, self.c_x, [()], self.c.start, self.c.size)
        self.final(mine)

    def finish(self):
        for key, copy in self.flights.items():
            if key[0] != "core" or key[1] not in self.released:
                copy.wait_send()


def scatter_scratch(block):
    dma = pltpu.SemaphoreType.DMA
    rows, lanes, kind = sum(b.shape[-2] for b in block), block[0].shape[-1], block[0].dtype
    a, b, c = (max(span.size, 16) for span in routes(rows))
    both = sum(span.size for span in routes(rows)[:2])
    return [
        pltpu.VMEM((4, 2, 2, rows, lanes), kind), pltpu.VMEM((4, 2, 2, rows, lanes), kind),
        pltpu.VMEM((4, 2, a, lanes), kind), pltpu.VMEM((4, 2, b, lanes), kind),
        pltpu.VMEM((4, both, lanes), kind), pltpu.VMEM((3, both, lanes), kind),
        pltpu.VMEM((3, 2, 2, c, lanes), kind), pltpu.VMEM((2, c, lanes), kind), pltpu.VMEM((c, lanes), kind),
        dma((11, 4)), dma((11, 4)), dma((4, 3)),
    ]


def in_order(plan, chain, networks):
    pieces = iter(chain)
    for item in plan:
        if item == -1:
            next(pieces)()
        else:
            networks[item[0]].run(item)
    assert next(pieces, None) is None and not any(net.todo for net in networks.values())


def small_rows(cond, forget, taps, place):
    at = lax.rem(place * taps.shape[0], LANES)
    taps = lax.dynamic_update_slice(jnp.zeros((4 * LANES,), bf16), taps, (at,)).reshape(4, LANES)
    cond = cond.reshape(-1, LANES)
    forget = forget.reshape(36, -1)
    return jnp.concatenate([
        jnp.pad(cond, ((0, 16 - cond.shape[0]), (0, 0))), jnp.pad(taps, ((0, 12), (0, 0))),
        jnp.pad(forget, ((0, 12), (0, LANES - forget.shape[1]))),
    ])


def unpack_small(small, taps_share, wf_ref, taps_ref, flat):
    wf_ref[: 32 * GROUPS, :] = small[:, 32:64, :].reshape(32 * GROUPS, LANES)
    wf_ref[32 * GROUPS :, :] = dot(pick_left(None, 0), small[:, 64:80, :].reshape(16 * GROUPS, LANES)).astype(bf16)
    flat[...] = jnp.zeros_like(flat)
    for d in range(GROUPS):
        row = d * taps_share // LANES
        flat[row : row + 4, :] += small[d, 16:32, :].astype(f32)[:4]
    tiles = taps_ref.shape[1] // LANES
    taps_ref[...] = jnp.zeros_like(taps_ref)
    for k in range(10):
        for t in range(tiles):
            taps_ref[k : k + 1, t * LANES : (t + 1) * LANES] = flat[k * tiles + t : k * tiles + t + 1, :]


def pack_rows(sources, wide, left, out):
    for j, (source, first, per_row) in enumerate(sources):
        if first == 0:
            wide[: source.shape[0], :] = source[...].astype(f32)
        for t in range(out.shape[1] // LANES):
            cols = slice(t * LANES, (t + 1) * LANES)
            rows = wide[pl.ds(first + t, 36, stride=per_row), :]
            out[32 * j : 32 * j + 32, cols] = rows[:32].astype(bf16)
            left[4 * j : 4 * j + 4, cols] = rows[32:]
    out[128:144, :] = left[...].astype(bf16)


def fill_permutation(perm_ref):
    width = perm_ref.shape[0]
    at = lax.broadcasted_iota(jnp.int32, (1, width), 1)
    late = at - 32 * GROUPS
    order = jnp.where(late < 0, (at >> 5) * 36 + (at & 31), (late >> 2) * 36 + 32 + (late & 3))
    for rows in spans(width, 2 * LANES):
        row = lax.broadcasted_iota(jnp.int32, (rows.stop - rows.start, width), 0) + rows.start
        perm_ref[rows, :] = (row == order).astype(bf16)


def forward_kernel(
    head_width, heads, taps_share, x_ref, ada_ref, bf_ref, own_s, query_ref, key_ref, value_ref, out_ref, up_ref,
    all_s, all_a, all_u, xp_out, qkv_out, mix_out, mixedp_out, branch_out, middle_out, h2p_out, perm_out,
    mod_ref, wf_ref, taps_ref, gate_ref, run_ref, runt_ref, state_ref, rims_ref, given_ref, taken_ref,
    xp_ref, qkv_ref, mix_ref, mixedp_ref, branch_ref, middle_ref, h2p_ref, perm_ref,
    own_a, own_u, wide, rows_left, small, flat, partial, main, left, outbox, inbox, vpad, mixed, load_sem, swap_sem, *rest,
):
    length, width = x_ref.shape
    tiles = width // LANES
    here = Here()
    lower = here.x == 0
    pack_rows([(ref, 0, tiles) for ref in (query_ref, key_ref, value_ref, out_ref)], wide, rows_left, own_a)
    pack_rows([(up_ref, j * tiles, 4 * tiles) for j in range(4)], wide, rows_left, own_u)
    first = Gather("f", here, (own_s,), (all_s,), rest[:3])
    gather = Gather("g", here, (own_a, own_u), (all_a, all_u), rest[3:6])

    def to_mod(total):
        for k in range(6):
            for t in range(tiles):
                mod_ref[k : k + 1, t * LANES : (t + 1) * LANES] = total[k * tiles + t : k * tiles + t + 1, :]
        mod_ref[6:8, :] = jnp.zeros((2, width), f32)

    scatter = Scatter("s", here, [partial], to_mod, rest[6:])
    stores, loads = [], []

    def fetch(number, source, target):
        copy = pltpu.make_async_copy(source, target, load_sem.at[number])
        copy.start()
        return copy

    def modulation():
        first.arrived(0)
        fetch(5, all_s, small).wait()
        me = ((here.z * 2 + here.y) * 2 + here.core) * 2 + here.x
        row = lax.broadcasted_iota(jnp.int32, (width, LANES), 0)
        lane = lax.broadcasted_iota(jnp.int32, (width, LANES), 1)
        pick = ((row == lane + me * 36) & (lane < 36)).astype(bf16)
        lines = small[...].reshape(GROUPS, 80, LANES)[:, :16, :].astype(f32)
        mine = jnp.zeros((GROUPS, LANES), f32)
        for t in range(tiles):
            cond = lines[:, t, :]
            cond = (cond / (1.0 + jnp.exp(-cond))).astype(bf16)
            mine = mine + dot(cond, pick[t * LANES : (t + 1) * LANES])
        lane = lax.broadcasted_iota(jnp.int32, mine.shape, 1)
        mine = jnp.where(lane == 36, 1.0, mine).astype(bf16)
        for t in range(6 * tiles):
            partial[:, t, :] = dot(mine, ada_ref[:, t * LANES : (t + 1) * LANES])
        partial[:, 6 * tiles :, :] = jnp.zeros((GROUPS, 64 - 6 * tiles, LANES), f32)
        scatter.prepare()
        scatter.start()

    def small_arrays():
        unpack_small(small[...].reshape(GROUPS, 80, LANES), taps_share, wf_ref, taps_ref, flat)

    def norm_one():
        first_part(x_ref, mod_ref, perm_ref, wf_ref, bf_ref, xp_ref, gate_ref, run_ref, runt_ref)
        stores.extend([fetch(6, xp_ref, xp_out), fetch(13, perm_ref, perm_out)])
        total = run_ref[0, length - 1 : length, :]
        given_ref[0] = jnp.where(lower, jnp.exp(total - run_ref[0]), jnp.exp(run_ref[1]))
        taken_ref[0] = jnp.where(lower, jnp.exp(total - run_ref[1]), jnp.exp(run_ref[0]))
        mix_ref[...] = jnp.zeros_like(mix_ref)

    def load(slot):
        loads.append(fetch(slot, all_a.at[:, :, :, :, pl.ds(32 * slot, 32)], main.at[slot % 2]))

    def project(slot):
        if slot == 0:
            gather.arrived(0)
            others = fetch(4, all_a.at[:, :, :, :, pl.ds(128, 16)], left)
            load(0)
            load(1)
            others.wait()
        loads[slot].wait()

        def write(cols, value):
            qkv_ref[slot, :, cols] = value.astype(bf16)

        project_part(slot, xp_ref, main.at[slot % 2], left, write)
        if slot < 2:
            load(slot + 2)
        else:
            stores.append(fetch(7, qkv_ref, qkv_out))

    def states():
        state_part(head_width, 1, lambda cols: qkv_ref[1, :, cols], qkv_ref.at[2], given_ref, outbox)
        edge = pl.multiple_of((1 - here.x) * (length - GRID), GRID)

        def write_edge(t, value):
            outbox[0, width + t * GRID : width + (t + 1) * GRID, :] = value

        edge_part(qkv_ref[2, pl.ds(edge, GRID), :], write_edge)
        stores.append(push(outbox, inbox, swap_sem.at[0], swap_sem.at[1], here.over_x))

    def mix(part):
        mix_part(head_width, heads, part * heads // 4, (part + 1) * heads // 4, qkv_ref, run_ref, runt_ref, mix_ref)

    def mixing():
        swap = stores.pop()
        swap.wait_recv()
        state_ref[0] = inbox[0, :width, :]
        for t in range(tiles):
            cols = slice(t * LANES, (t + 1) * LANES)
            rows = inbox[0, width + t * GRID : width + (t + 1) * GRID, :]
            rims_ref[0, :, cols] = jnp.where(lower, 0, rows).astype(bf16)
            rims_ref[1, :, cols] = jnp.where(lower, rows, 0).astype(bf16)
        fill_padded(vpad, rims_ref, qkv_ref[2])
        mixed_part(head_width, 1, qkv_ref, taken_ref, state_ref, taps_ref, vpad, mix_ref, mixed)
        stores.append(fetch(8, mix_ref, mix_out))
        swap.wait_send()

    def turn():
        permute_part(mixed, perm_ref, mixedp_ref)
        stores.append(fetch(9, mixedp_ref, mixedp_out))

    def branch():
        loads[3].wait()
        branch_part(x_ref, mod_ref, mixedp_ref, main.at[1], left, branch_ref, middle_ref)
        stores.extend([fetch(10, branch_ref, branch_out), fetch(11, middle_ref, middle_out)])

    def norm_two():
        second_hidden(mod_ref, middle_ref, mixed)
        permute_part(mixed, perm_ref, h2p_ref)
        stores.append(fetch(12, h2p_ref, h2p_out))

    chain = [functools.partial(fill_permutation, perm_ref), modulation, small_arrays, norm_one]
    chain += [functools.partial(project, slot) for slot in range(3)] + [states]
    chain += [functools.partial(mix, part) for part in range(4)] + [mixing, turn, branch, norm_two]
    first.start()
    gather.start()
    here.greet()
    in_order(FORWARD_PLAN, chain, {"f": first, "g": gather, "s": scatter})
    gather.arrived(1)
    for network in (first, gather, scatter):
        network.finish()
    for copy in stores:
        copy.wait()


def forward_fused(x, ada, bf, small, shards, heads, taps_share):
    length, width = x.shape
    head_width = width // heads
    message = width + width // LANES * GRID
    anywhere, vm = pl.BlockSpec(memory_space=pl.ANY), pl.BlockSpec(memory_space=pltpu.VMEM)
    rows, wide = (length, width), (length, LANES)
    bulk = (
        sds(rows, bf16), sds((3,) + rows, bf16), sds(rows), sds(rows, bf16), sds(rows, bf16), sds(rows), sds(rows, bf16),
        sds((width, width), bf16),
    )
    kept = (
        sds((8, width)), sds((width, LANES), bf16), sds((16, width)), sds(wide), sds((2,) + wide), sds((2, LANES, length)),
        sds((1, width, LANES), bf16), sds((2, GRID, width), bf16), sds((1,) + wide), sds((1,) + wide),
    )
    partial = sds((GROUPS, 64, LANES))
    own = sds((144, width), bf16)
    dma = pltpu.SemaphoreType.DMA
    out = pl.pallas_call(
        functools.partial(forward_kernel, head_width, heads, taps_share),
        out_shape=tuple(gathered_shape(b) for b in (small, own, own)) + bulk + kept,
        in_specs=[vm] * 9,
        out_specs=(anywhere,) * (3 + len(bulk)) + (vm,) * len(kept),
        scratch_shapes=[pltpu.VMEM(b.shape, b.dtype) for b in bulk] + [
            pltpu.VMEM(own.shape, bf16), pltpu.VMEM(own.shape, bf16), pltpu.VMEM(shards[4].shape, f32),
            pltpu.VMEM((16, width), f32),
            pltpu.VMEM((4, 2, 2, 2) + small.shape, bf16), pltpu.VMEM((96, LANES), f32),
            pltpu.VMEM(partial.shape, f32), pltpu.VMEM((2, 4, 2, 2, 2, 32, width), bf16),
            pltpu.VMEM((4, 2, 2, 2, 16, width), bf16), pltpu.VMEM((1, message, LANES), bf16),
            pltpu.VMEM((1, message, LANES), bf16), pltpu.VMEM((length + 2 * GRID, width), bf16), pltpu.VMEM(rows, bf16),
            dma((14,)), dma((2,)),
        ] + gather_sems(1) + gather_sems(2) + scatter_scratch([partial]),
        compiler_params=pltpu.CompilerParams(collective_id=0, has_side_effects=True, vmem_limit_bytes=VMEM_LIMIT),
        name="forward",
    )(x, ada, bf, small, *shards)
    gathered = [g.reshape((GROUPS,) + g.shape[4:]) for g in out[:3]]
    return gathered, out[3 : 3 + len(bulk)], out[3 + len(bulk) :]


def feed_fused_kernel(
    h2p, cot, mod_ref, flat_d, up_in, middle_in,
    all_d, out_out, gh_out, gup_out, gleft_ref, ggate_ref, down_own,
    gdi, h2pt, act, slope, actt, gup, main, left, left_own, down, down_acc, gh, stage_d, stage_u, own_d, wide, load_sem, *rest,
):
    length, width = h2p.shape
    main_rows = GROUPS * 32
    here = Here()
    gather = Gather("g", here, (own_d,), (all_d,), rest[:3])
    scatter = Scatter("d", here, [stage_d], plain_final(down_own), rest[3:])
    order = [here.ring_z(k + 1) for k in range(4)]

    def fetch(number, source, target):
        copy = pltpu.make_async_copy(source, target, load_sem.at[number])
        copy.start()
        return copy

    def load_up(k, number):
        rows = pl.ds(pl.multiple_of(32 * order[k], 32), 32)
        return fetch(number, up_in.at[:, rows], main.at[k % 2])

    def load_down(k):
        gather.arrived(0, [(k + 1) % 4])
        return fetch(8 + k, all_d.at[order[k]], down.at[k % 2])

    def left_rows(k):
        return dot(pick_left(None, order[k]), left[...].reshape(16 * GROUPS, width)).astype(bf16)

    def start():
        gdi[...] = (cot[...].astype(f32) * mod_ref[5:6, :]).astype(bf16)
        h2pt[...] = h2p[...].T
        gleft_ref[...] = jnp.zeros_like(gleft_ref)
        others.wait()

    def up_step(k):
        loads[k].wait()
        left_own[...] = left_rows(k)
        for cols in spans(width):
            up = dot(h2p[:, :main_rows], main[k % 2, :, :, cols].reshape(main_rows, -1))
            up = up + dot(h2p[:, main_rows:], left_own[:, cols])
            value, rate = gelu_both(up)
            value = value.astype(bf16)
            act[k, :, cols] = value
            actt[cols, :] = value.T
            slope[k, :, cols] = rate.astype(bf16)
        loads.append(load_up(k + 2, k + 2) if k < 2 else load_up(k - 2, k + 2))

    def down_grad(k):
        if k > 0:
            scatter.release(k - 1)
        for cols in spans(width):
            stage_d[:, :, :, :, cols] = dot(actt[...], gdi[:, cols]).astype(bf16).reshape(2, 2, 2, width // 8, -1)
        scatter.offer(k)

    def back_act(k):
        load_down(k).wait()
        rows_of = down[k % 2].reshape(width, width)
        for cols in spans(width):
            gup[:, cols] = (dot_bt(gdi[...], rows_of[cols]) * slope[k, :, cols].astype(f32)).astype(bf16)

    def down_step(k):
        rows_of = down[k % 2].reshape(width, width)
        for cols in spans(width):
            part = dot(act[k], rows_of[:, cols])
            if k == 0:
                down_acc[:, cols] = part
            else:
                down_acc[:, cols] += part
    def back_hidden(k):
        loads[4 + k].wait()
        for cols in spans(main_rows):
            part = dot_bt(gup[...], main[k % 2, cols.start // 32 : cols.stop // 32].reshape(-1, width))
            if k == 0:
                gh[:, cols] = part
            else:
                gh[:, cols] += part
        part = dot_bt(gup[...], left_rows(k))
        if k == 0:
            gh[:, main_rows:] = part
        else:
            gh[:, main_rows:] += part
        if k < 2:
            loads.append(load_up(k + 2, 6 + k))

    def up_grad(k):
        if k > 0:
            stores[k - 1].wait()
        projection_grads(order[k], h2pt, gup, stage_u, gleft_ref)
        rows = pl.ds(pl.multiple_of(32 * order[k], 32), 32)
        stores.append(fetch(13 + k, stage_u, gup_out.at[:, rows]))

    def end():
        keep = fetch(17, gh, gh_out)
        ggate_ref[...] = jnp.sum(cot[...].astype(f32) * down_acc[...], axis=0, keepdims=True)
        keep.wait()
        fetch(18, middle_in, gh).wait()
        for cols in spans(width):
            act[0, :, cols] = (gh[:, cols] + mod_ref[5:6, cols] * down_acc[:, cols]).astype(bf16)
        stores.append(fetch(19, act.at[0], out_out))

    chain = [start]
    for k in range(4):
        chain += [functools.partial(up_step, k), functools.partial(down_grad, k)]
    for k in range(4):
        chain += [functools.partial(step, k) for step in (back_act, down_step, back_hidden, up_grad)]
    others = fetch(12, up_in.at[:, pl.ds(128, 16)], left)
    loads = [load_up(0, 0), load_up(1, 1)]
    stores = []
    wide[...] = flat_d[...].astype(f32)
    for t in range(width // LANES):
        rows = wide[pl.ds(t, own_d.shape[0], stride=width // LANES), :]
        own_d[:, t * LANES : (t + 1) * LANES] = rows.astype(bf16)
    gather.start()
    here.greet()
    in_order(FEED_PLAN, chain + [end], {"d": scatter, "g": gather})
    scatter.finish()
    gather.finish()
    stores[3].wait()
    stores[4].wait()


def feed_fused(h2p, cot, mod, flat_d, up_w, middle):
    length, width = h2p.shape
    anywhere, vm = pl.BlockSpec(memory_space=pl.ANY), pl.BlockSpec(memory_space=pltpu.VMEM)
    rows = (length, width)
    dma = pltpu.SemaphoreType.DMA
    stage = (2, 2, 2, width // 8, width)
    own = sds((width // 8, width), bf16)
    return pl.pallas_call(
        feed_fused_kernel,
        out_shape=(
            gathered_shape(own), sds(rows, bf16), sds(rows), sds((GROUPS, 128, width), bf16),
            sds((GROUPS, 16, width), bf16), sds((1, width)), sds(flat_d.shape),
        ),
        in_specs=[vm] * 4 + [anywhere] * 2,
        out_specs=(anywhere,) * 4 + (vm,) * 3,
        scratch_shapes=[
            pltpu.VMEM(rows, bf16), pltpu.VMEM((width, length), bf16), pltpu.VMEM((4,) + rows, bf16),
            pltpu.VMEM((4,) + rows, bf16), pltpu.VMEM((width, length), bf16), pltpu.VMEM(rows, bf16),
            pltpu.VMEM((2, GROUPS, 32, width), bf16), pltpu.VMEM((GROUPS, 16, width), bf16), pltpu.VMEM((128, width), bf16),
            pltpu.VMEM((2,) + stage, bf16), pltpu.VMEM(rows, f32), pltpu.VMEM(rows, f32), pltpu.VMEM(stage, bf16),
            pltpu.VMEM((GROUPS, 32, width), bf16), pltpu.VMEM(own.shape, bf16), pltpu.VMEM(flat_d.shape, f32), dma((20,)),
        ] + gather_sems(1) + scatter_scratch([sds(stage, bf16)]),
        compiler_params=pltpu.CompilerParams(
            collective_id=1, has_side_effects=True, vmem_limit_bytes=62 * 1024 * 1024
        ),
        name="feed",
    )(h2p, cot, mod, flat_d, up_w, middle)[1:]


def six(array):
    return array.reshape((4, 2, 2, 2) + array.shape[1:])


def flat_rows(out, first, value, per_row):
    for t in range(value.shape[1] // LANES):
        out[pl.ds(first + t, value.shape[0], stride=per_row), :] = value[:, t * LANES : (t + 1) * LANES]


def square_final(outs):
    def final(total):
        value = total[...].astype(f32)
        per_row = value.shape[1] // LANES
        for j, out in enumerate(outs):
            flat_rows(out, 0, value[32 * j : 32 * j + 32], per_row)
            flat_rows(out, 32 * per_row, value[128 + 4 * j : 132 + 4 * j], per_row)

    return final


def columns_final(out):
    def final(total):
        value = total[...].astype(f32)
        tiles = value.shape[1] // LANES
        for j in range(4):
            flat_rows(out, j * tiles, value[32 * j : 32 * j + 32], 4 * tiles)
            flat_rows(out, 32 * 4 * tiles + j * tiles, value[128 + 4 * j : 132 + 4 * j], 4 * tiles)

    return final


def plain_final(out):
    def final(total):
        value = total[...].astype(f32)
        flat_rows(out, 0, value, value.shape[1] // LANES)

    return final


def small_final(out):
    def final(total):
        out[...] = total[...]

    return final


def fill_small(block, gforget, conv, bias, flat, taps_share):
    tiles = conv.shape[1] // LANES
    for k in range(10):
        for t in range(tiles):
            flat[k * tiles + t : k * tiles + t + 1, :] = conv[k : k + 1, t * LANES : (t + 1) * LANES]
    flat[10 * tiles :, :] = jnp.zeros_like(flat[10 * tiles :, :])
    block[:, :32, :] = gforget[: 32 * GROUPS, :].reshape(GROUPS, 32, LANES)
    block[:, 40:, :] = jnp.broadcast_to(bias[...].reshape(1, 1, LANES), (GROUPS, 8, LANES))
    for d in range(GROUPS):
        at = 32 * GROUPS + 4 * d
        block[d, 32:36, :] = gforget[at : at + 4, :]
        row = d * taps_share // LANES
        block[d, 36:40, :] = flat[row : row + 4, :]


def backward_kernel(
    head_width, heads, taps_share,
    mod_ref, run_ref, runt_ref, taken_ref, given_ref, gate_ref, state_ref, vrims_ref, taps_ref,
    ghp_in, perm_in, middle_in, cot_in, branch_in, mixedp_in, mix_in, weight_in, qkv_in, xp_in, gup_in, gupl_in,
    gmid_out, gqkv_out, gmain_out, gout_out, small_out, gleft_ref, ggate_ref, sums_ref, up_ref,
    pool, perm, gmixed, gmix, gb, turned, main, left, qkv, gqkv, held, vpad, gpad, pair_rows, pair_cols,
    outbox, inbox, rims, leave, conv_ref, bias_ref, gforget_ref, flat, small, fetch_sem, swap_sem, *scratch,
):
    length, width = gmix.shape
    here = Here()
    lower = here.x == 0
    scatter = Scatter("u", here, [gup_in, gupl_in], columns_final(up_ref), scratch)
    scatter.prepare()

    def fetch(number, source, target):
        copy = pltpu.make_async_copy(source, target, fetch_sem.at[number])
        copy.start()
        return copy

    first = [
        fetch(0, ghp_in, pool.at[0]), fetch(1, perm_in, perm), fetch(2, middle_in, pool.at[1]), fetch(3, cot_in, qkv.at[0]),
        fetch(4, branch_in, qkv.at[1]), fetch(5, mixedp_in, qkv.at[2]),
        fetch(6, weight_in.at[:, pl.ds(96, 32)], main.at[0]), fetch(7, weight_in.at[:, pl.ds(128, 16)], left),
        fetch(8, mix_in, pool.at[2]),
    ]
    second = second_part(
        head_width, pool.at[0], perm, pool.at[1], mod_ref, qkv.at[0], qkv.at[1], qkv.at[2], pool.at[2], main.at[0], left,
        pool.at[1], gmixed, gmix, main.at[1], gleft_ref, sums_ref, pool.at[3], gb, turned,
    )
    gq, gk, gv = pool.at[0], pool.at[2], pool.at[3]
    early = jnp.where(lower, jnp.ones((1, LANES), f32), 0.0)
    carry = carry_part(
        head_width, 1, early, qkv, gmix, gq, gk, gv, pair_rows, pair_cols, taken_ref, given_ref, gate_ref, state_ref,
        leave, jnp.zeros((1, LANES), f32), vpad, gpad, taps_ref, gqkv, ggate_ref, conv_ref, bias_ref,
    )
    stores = []

    def begin():
        for copy in first:
            copy.wait()
        next(second)

    def states():
        again = fetch(9, qkv_in, qkv)
        stores.extend([fetch(10, pool.at[1], gmid_out), fetch(11, main.at[1], gout_out), fetch(12, xp_in, gb)])
        for ref in (gq, gk, gv, pair_rows, pair_cols):
            ref[...] = jnp.zeros_like(ref)
        again.wait()
        state_part(head_width, 1, lambda cols: qkv[0, :, cols], gmix, taken_ref, outbox)
        edge = pl.multiple_of((1 - here.x) * (length - GRID), GRID)

        def write_edge(t, value):
            outbox[0, width + t * GRID : width + (t + 1) * GRID, :] = value

        edge_part(gmixed[pl.ds(edge, GRID), :], write_edge)
        stores.append(push(outbox, inbox, swap_sem.at[0], swap_sem.at[1], here.over_x))

    def pairs(part):
        pairs_part(
            head_width, heads, part * heads // 4, (part + 1) * heads // 4, qkv, gmix, run_ref, runt_ref, gq, gk, gv,
            pair_rows, pair_cols, held,
        )

    def carry_first():
        swap = stores.pop()
        swap.wait_recv()
        leave[0] = inbox[0, :width, :]
        for t in range(width // LANES):
            cols = slice(t * LANES, (t + 1) * LANES)
            edge_rows = inbox[0, width + t * GRID : width + (t + 1) * GRID, :]
            rims[0, :, cols] = jnp.where(lower, 0, edge_rows).astype(bf16)
            rims[1, :, cols] = jnp.where(lower, edge_rows, 0).astype(bf16)
        fill_padded(vpad, vrims_ref, qkv[2])
        fill_padded(gpad, rims, gmixed[...])
        next(carry)
        swap.wait_send()

    def turn():
        stores.append(fetch(13, gqkv, gqkv_out))
        stores[2].wait()
        turned[...] = gb[...].T
        gforget_ref[...] = dot(turned[...], ggate_ref[...])
        fill_small(small, gforget_ref, conv_ref, bias_ref, flat, taps_share)
        fetch(17, small, small_out).wait()

    def weight(slot):
        buffer = main.at[slot % 2]
        if slot == 1:
            stores[1].wait()
        if slot == 2:
            stores[4].wait()
        projection_grads(slot, turned, gqkv.at[slot], buffer, gleft_ref)
        stores.append(fetch(14 + slot, buffer, gmain_out.at[:, pl.ds(32 * slot, 32)]))

    chain = [begin] + [functools.partial(next, second)] * 3 + [states]
    chain += [functools.partial(pairs, part) for part in range(4)] + [carry_first]
    chain += [functools.partial(next, carry)] * 3 + [turn] + [functools.partial(weight, slot) for slot in range(3)]
    here.greet()
    scatter.start()
    in_order(BACKWARD_PLAN, chain, {"u": scatter})
    scatter.finish()
    for number in (0, 3, 5, 6):
        stores[number].wait()


def backward_fused(heads, taps_share, small, arrays, grads):
    length, width = arrays[0].shape
    head_width = width // heads
    message = width + width // LANES * GRID
    anywhere, vm = pl.BlockSpec(memory_space=pl.ANY), pl.BlockSpec(memory_space=pltpu.VMEM)
    rows, wide = (length, width), (length, LANES)
    dma = pltpu.SemaphoreType.DMA
    return pl.pallas_call(
        functools.partial(backward_kernel, head_width, heads, taps_share),
        out_shape=(
            sds(rows), sds((3,) + rows, bf16), sds((GROUPS, 96, width), bf16), sds((GROUPS, 32, width), bf16),
            sds((GROUPS, 48, LANES)), sds((GROUPS, 16, width), bf16), sds(wide, bf16), sds((8, width)),
            sds((144 * width // LANES, LANES)),
        ),
        in_specs=[vm] * len(small) + [anywhere] * (len(arrays) + len(grads)),
        out_specs=(anywhere,) * 5 + (vm,) * 4,
        scratch_shapes=[
            pltpu.VMEM((4,) + rows, f32), pltpu.VMEM((width, width), bf16), pltpu.VMEM(rows, bf16), pltpu.VMEM(rows, bf16),
            pltpu.VMEM(rows, bf16), pltpu.VMEM((width, length), bf16),
            pltpu.VMEM((2, GROUPS, 32, width), bf16), pltpu.VMEM((GROUPS, 16, width), bf16), pltpu.VMEM((3,) + rows, bf16),
            pltpu.VMEM((3,) + rows, bf16), pltpu.VMEM((2, length, length), bf16),
            pltpu.VMEM((length + 2 * GRID, width), bf16), pltpu.VMEM((length + 2 * GRID, width), bf16),
            pltpu.VMEM((2,) + wide, f32), pltpu.VMEM((2, heads, length), f32),
            pltpu.VMEM((1, message, LANES), bf16), pltpu.VMEM((1, message, LANES), bf16),
            pltpu.VMEM((2, GRID, width), bf16), pltpu.VMEM((1, width, LANES), bf16), pltpu.VMEM((16, width), f32),
            pltpu.VMEM((1, LANES), f32), pltpu.VMEM((width, LANES), f32), pltpu.VMEM((96, LANES), f32),
            pltpu.VMEM((GROUPS, 48, LANES), f32), dma((18,)), dma((2,)),
        ] + scatter_scratch(grads),
        compiler_params=pltpu.CompilerParams(
            collective_id=3, has_side_effects=True, vmem_limit_bytes=62 * 1024 * 1024
        ),
        name="backward",
    )(*small, *arrays, *[six(g) for g in grads])


def finish_kernel(
    mod_ref, sums_two, gate_two, ggate_ref, wf_ref,
    weight_in, gqkv_in, perm_in, x_in, gmid_in, gmain_in, gout_in, gleft_in, small_in,
    gin_ref, all_mod, query_ref, key_ref, value_ref, out_ref, small_ref,
    main, left, gqkv, perm, x, gmid, ghp, gh, sums_one, own_mod, load_sem, *rest,
):
    width = perm.shape[0]
    here = Here()
    scatter = Scatter(
        "a", here, [gmain_in, gout_in, gleft_in], square_final((query_ref, key_ref, value_ref, out_ref)), rest[:12]
    )
    small = Scatter("s", here, [small_in], small_final(small_ref), rest[12:24])
    gather = Gather("g", here, (own_mod,), (all_mod,), rest[24:])
    scatter.prepare()
    small.prepare()

    def fetch(number, source, target):
        copy = pltpu.make_async_copy(source, target, load_sem.at[number])
        copy.start()
        return copy

    def load(slot):
        return fetch(slot, weight_in.at[:, pl.ds(32 * slot, 32)], main.at[slot % 2])

    grads = fetch(3, gqkv_in, gqkv)
    rest_rows = fetch(4, weight_in.at[:, pl.ds(128, 16)], left)
    loads = [load(0), load(1)]
    others = [fetch(5, perm_in, perm), fetch(6, x_in, x), fetch(7, gmid_in, gmid)]

    def back(slot):
        if slot == 0:
            ghp[...] = dot_bt(ggate_ref[...], wf_ref[...])
            grads.wait()
            rest_rows.wait()
        loads[slot].wait()
        projection_back(slot, gqkv.at[slot], main.at[slot % 2], left, ghp)
        if slot == 0:
            loads.append(load(2))

    def last():
        for copy in others:
            copy.wait()
        last_part(ghp, perm, x, mod_ref, gmid, gin_ref, sums_one, gh)
        lines = [sums_one[0:1, :], sums_one[1:2, :], sums_two[2:3, :], sums_two[0:1, :], sums_two[1:2, :], gate_two[...]]
        tiles = width // LANES
        for k, line in enumerate(lines):
            for t in range(tiles):
                own_mod[k * tiles + t : k * tiles + t + 1, :] = line[:, t * LANES : (t + 1) * LANES]
        own_mod[len(lines) * tiles :, :] = jnp.zeros_like(own_mod[len(lines) * tiles :, :])
        gather.start()

    here.greet()
    scatter.start()
    small.start()
    chain = [functools.partial(back, slot) for slot in range(3)] + [last]
    in_order(FINISH_PLAN, chain, {"a": scatter, "s": small, "g": gather})
    gather.arrived(0)
    for network in (scatter, small, gather):
        network.finish()


def finish_fused(small, arrays, grads, grad_small):
    length, width = arrays[3].shape
    anywhere, vm = pl.BlockSpec(memory_space=pl.ANY), pl.BlockSpec(memory_space=pltpu.VMEM)
    rows = (length, width)
    dma = pltpu.SemaphoreType.DMA
    own = sds((64, LANES))
    return pl.pallas_call(
        finish_kernel,
        out_shape=(sds(rows), gathered_shape(own)) + (sds((36 * width // LANES, LANES)),) * 4 + (sds(grad_small.shape[1:]),),
        in_specs=[vm] * len(small) + [anywhere] * (len(arrays) + len(grads) + 1),
        out_specs=(vm, anywhere) + (vm,) * 5,
        scratch_shapes=[
            pltpu.VMEM((2, GROUPS, 32, width), bf16), pltpu.VMEM((GROUPS, 16, width), bf16), pltpu.VMEM((3,) + rows, bf16),
            pltpu.VMEM((width, width), bf16), pltpu.VMEM(rows, bf16), pltpu.VMEM(rows, f32), pltpu.VMEM(rows, f32),
            pltpu.VMEM(rows, f32), pltpu.VMEM((8, width), f32), pltpu.VMEM(own.shape, f32), dma((8,)),
        ] + scatter_scratch(grads) + scatter_scratch([grad_small]) + gather_sems(1),
        compiler_params=pltpu.CompilerParams(
            collective_id=4, has_side_effects=True, vmem_limit_bytes=VMEM_LIMIT
        ),
        name="finish",
    )(*small, *arrays, *[six(g) for g in grads], six(grad_small))


def joined_states(messages, totals, width, head_width):
    count = lax.axis_size("seq")
    place = lax.axis_index("seq")

    def grid_rows(message):
        rows = message[width:].reshape(width // LANES, GRID, LANES)
        return rows.transpose(1, 0, 2).reshape(GRID, width)

    if count == 1:
        return jnp.zeros_like(messages[:, :width]), jnp.zeros((2, GRID, width), bf16)
    if count == 2:
        got = lax.ppermute(messages[0], "seq", [(0, 1), (1, 0)])
        rows = grid_rows(got)
        return got[None, :width], jnp.stack([jnp.where(place == 1, rows, 0), jnp.where(place == 0, rows, 0)])
    forward = [(i, i + 1) for i in range(count - 1)]
    backward = [(i + 1, i) for i in range(count - 1)]
    rims = jnp.stack([
        grid_rows(lax.ppermute(messages[0], "seq", forward)), grid_rows(lax.ppermute(messages[1], "seq", backward))
    ])
    states = lax.all_gather(messages[:, :width, :], "seq").astype(f32)
    passed = lax.all_gather(totals, "seq")
    heads_of_rows = np.arange(width) // head_width
    order = jnp.arange(count)
    ahead = jnp.zeros(states.shape[2:], f32)
    behind = jnp.zeros(states.shape[2:], f32)
    for source in range(count):
        between_up = jnp.where((order > source) & (order < place), 1.0, 0.0) @ passed
        between_down = jnp.where((order < source) & (order > place), 1.0, 0.0) @ passed
        ahead = ahead + jnp.where(source < place, jnp.exp(between_up), 0.0)[heads_of_rows, None] * states[source, 0]
        behind = behind + jnp.where(source > place, jnp.exp(between_down), 0.0)[heads_of_rows, None] * states[source, 1]
    return jnp.stack([ahead, behind]).astype(bf16), rims


def split_rows(matrix):
    grouped = matrix.reshape(GROUPS, -1, matrix.shape[1])
    return grouped[:, :32], grouped[:, 32:]


def pack_whole(parts, width):
    query, key, value, out, up, down = parts
    square = [piece.reshape(GROUPS, -1, width) for piece in (query, key, value, out)]
    up = up.reshape(GROUPS, square[0].shape[1], -1, width)
    columns = [up[:, :, j] for j in range(up.shape[2])]
    blocks = []
    for group in (square, columns):
        blocks.append(
            jnp.concatenate([piece[:, :32] for piece in group] + [piece[:, 32:] for piece in group], axis=1)
        )
    return blocks + [down.reshape(GROUPS, -1, width)]


def unpack_squares(block):
    return [
        jnp.concatenate([block[..., 32 * j : 32 * j + 32, :], block[..., 128 + 4 * j : 132 + 4 * j, :]], axis=-2)
        for j in range(4)
    ]


def unpack_blocks(blocks):
    squares = unpack_squares(blocks[0])
    columns = unpack_squares(blocks[1])
    lead = blocks[0].shape[:-2]
    up = jnp.stack(columns, axis=-2)
    return [piece.reshape(lead + (-1,)) for piece in squares] + [up.reshape(lead + (-1,)), blocks[2].reshape(lead + (-1,))]


def on_device(
    activations, conditioning, cotangent, w_ada, b_ada, w_query, w_key, w_value, w_forget, b_forget, conv_taps, w_out,
    w_up, w_down,
):
    _, length, width = activations.shape
    heads = b_forget.shape[0]
    head_width = width // heads
    data_count, seq_count = lax.axis_size("dp"), lax.axis_size("seq")
    devices = data_count * seq_count
    me = lax.axis_index("dp") * seq_count + lax.axis_index("seq")
    packed_here = (data_count, seq_count) == (16, 2)
    everywhere = ("dp", "seq")

    mod_width = 6 * width
    share = w_ada.shape[0]
    if share % mod_width == 0:
        ada_rows = share // mod_width
        first_row, inset = me * ada_rows, None
        ada_part = w_ada.reshape(ada_rows, mod_width)
    else:
        ada_rows = -(-share // mod_width) + 1
        first_row = (me * share) // mod_width
        inset = me * share - first_row * mod_width
        ada_part = lax.dynamic_update_slice(jnp.zeros((ada_rows * mod_width,), bf16), w_ada, (inset,))
        ada_part = ada_part.reshape(ada_rows, mod_width)

    def own_columns(cond_all):
        cond_act = jax.nn.silu(cond_all.astype(f32)).astype(bf16)
        cond_wide = jnp.pad(cond_act, ((0, 0), (0, ada_rows)))
        return lax.dynamic_slice_in_dim(cond_wide, first_row, ada_rows, axis=1)

    main_rows = 32 * GROUPS
    forget_b = jnp.pad(b_forget.astype(f32), (0, LANES - heads)).reshape(1, LANES)
    x = activations[0]
    cot = cotangent[0]
    rows = (length, width)

    def main_spec(block, columns=width):
        return pl.BlockSpec((GROUPS, 32, columns), block)

    def left_spec(block, columns=width):
        return pl.BlockSpec((GROUPS, 16, columns), block)

    def whole(shape):
        return pl.BlockSpec(shape, lambda *_: (0,) * len(shape))

    ways = 1 if seq_count == 2 else 2
    message_rows = width + width // LANES * GRID
    state_call = call(
        functools.partial(state_kernel, head_width, ways), sds((ways, message_rows, LANES), bf16), "states"
    )
    place = lax.axis_index("seq")

    def edges(values):
        low, high = values[:GRID], values[-GRID:]
        if ways == 1:
            return jnp.where(place == 0, high, low)[None]
        return jnp.stack([high, low])

    shards = (w_query, w_key, w_value, w_out, w_up, w_down)
    if packed_here:
        small = small_rows(conditioning[0], w_forget, conv_taps, me)
        bias_row = lax.dynamic_update_slice(jnp.zeros((1, mod_width), bf16), b_ada[None], (0, me * b_ada.shape[0]))
        ada = jnp.pad(jnp.concatenate([ada_part, bias_row]), ((0, LANES - 1 - ada_rows), (0, 0)))
        (small, attention_w, up_w), bulk, kept = forward_fused(
            x, ada, forget_b, small, [piece.reshape(-1, LANES) for piece in shards[:5]], heads, conv_taps.shape[0]
        )
        xp, qkv, mix, mixed_p, branch, middle, hidden_two_p, perm = bulk
        mod, forget_p, taps, gate_pre, run, runt, states, value_rims, given, taken = kept
        cond_part = own_columns(small[::seq_count, : width // LANES, :].reshape(data_count, width))
        output, ghp_two, gup_main, gup_left, ggate_two, g_down = feed_fused(
            hidden_two_p, cot, mod, w_down.reshape(-1, LANES), up_w, middle
        )
    else:
        lanes_at = np.arange(width)
        per_group = width // GROUPS
        order = np.where(
            lanes_at < main_rows,
            lanes_at // 32 * per_group + lanes_at % 32,
            (lanes_at - main_rows) // 4 * per_group + 32 + (lanes_at - main_rows) % 4,
        )
        perm = (jnp.arange(width, dtype=jnp.int32)[:, None] == jnp.asarray(order, jnp.int32)[None, :]).astype(bf16)
        small = [w_forget, conv_taps, b_ada]
        sizes = np.cumsum([0] + [piece.shape[0] for piece in small])
        small = lax.all_gather(jnp.concatenate(small), everywhere)
        forget_w = small[:, : sizes[1]].reshape(width, heads)
        taps = small[:, sizes[1] : sizes[2]].reshape(10, width).astype(f32)
        taps = jnp.pad(taps, ((0, 6), (0, 0)))
        ada_bias = small[:, sizes[2] :].reshape(6, width).astype(f32)
        forget_main, forget_left = split_rows(forget_w)
        forget_p = jnp.concatenate([forget_main.reshape(-1, heads), forget_left.reshape(-1, heads)])
        forget_p = jnp.pad(forget_p, ((0, 0), (0, LANES - heads)))
        cond_part = own_columns(lax.all_gather(conditioning, "dp", axis=0, tiled=True))
        partial_mod = jnp.dot(cond_part, ada_part, preferred_element_type=f32)
        mod = lax.psum(lax.psum_scatter(partial_mod, "dp", scatter_dimension=0, tiled=True), "seq")
        mod = jnp.pad(mod.reshape(6, width) + ada_bias, ((0, 2), (0, 0)))
        blocks = pack_whole([lax.all_gather(s, everywhere, axis=0, tiled=True) for s in shards], width)
        attention_w, up_w, down_w = blocks
        down_w = down_w.reshape(-1, width)
        xp, gate_pre, run, runt = call(
            first_part,
            (sds(rows, bf16), sds((length, LANES)), sds((2, length, LANES)), sds((2, LANES, length))),
            "first_norm",
        )(x, mod, perm, forget_p, forget_b)
        qkv = call(
            project_kernel,
            sds((3,) + rows, bf16),
            "project",
            grid=(3,),
            in_specs=[whole(rows), main_spec(lambda j: (0, j, 0)), left_spec(lambda j: (0, 8, 0))],
            out_specs=pl.BlockSpec((1,) + rows, lambda j: (j, 0, 0)),
        )(xp, attention_w, attention_w)
        total = run[0, -1]
        given = jnp.stack([jnp.exp(total - run[0]), jnp.exp(run[1])])
        taken = jnp.stack([jnp.exp(run[0]), jnp.exp(total - run[1])])
        if ways == 1:
            given = jnp.where(place == 0, given[0], given[1])[None]
            taken = jnp.where(place == 0, taken[1], taken[0])[None]
        messages = state_call(qkv[1], qkv[2], given, edges(qkv[2]))
        states, value_rims = joined_states(messages, total, width, head_width)
        mix_local = call(
            functools.partial(mix_kernel, head_width, heads), sds(rows), "mix"
        )(qkv, run, runt)
        mix, mixed_p, branch, middle, hidden_two_p = call(
            functools.partial(after_kernel, head_width, ways),
            (sds(rows), sds(rows, bf16), sds(rows, bf16), sds(rows), sds(rows, bf16)),
            "after",
            grid=(1,),
            in_specs=[
                whole(rows), whole((8, width)), whole((width, width)), whole((3,) + rows), whole(rows),
                whole((ways, length, LANES)), whole((ways, width, LANES)), whole((2, GRID, width)), whole((16, width)),
                main_spec(lambda i: (0, 3, 0)), left_spec(lambda i: (0, 8, 0)),
            ],
            out_specs=[whole(rows)] * 5,
            scratch_shapes=[pltpu.VMEM((length + 2 * GRID, width), bf16), pltpu.VMEM(rows, bf16)],
        )(x, mod, perm, qkv, mix_local, taken, states, value_rims, taps, attention_w, attention_w)
        output, ghp_two, gup_main, gup_left, gdown, ggate_two = call(
            feed_kernel,
            (
                sds(rows, bf16), sds(rows), sds((GROUPS, 128, width), bf16), sds((GROUPS, 16, width), bf16),
                sds(down_w.shape, bf16), sds((1, width)),
            ),
            "feed",
            grid=(4,),
            in_specs=[
                whole(rows), whole(rows), whole((8, width)), whole(rows), main_spec(lambda j: (0, j, 0)),
                left_spec(lambda j: (0, 8, 0)), pl.BlockSpec((width, width), lambda j: (j, 0)),
            ],
            out_specs=[
                whole(rows), whole(rows), main_spec(lambda j: (0, j, 0)), left_spec(lambda j: (0, 0, 0)),
                pl.BlockSpec((width, width), lambda j: (j, 0)), whole((1, width)),
            ],
            scratch_shapes=[
                pltpu.VMEM(rows, f32), pltpu.VMEM(rows, bf16), pltpu.VMEM((width, length), bf16), pltpu.VMEM(rows, bf16),
                pltpu.VMEM((width, length), bf16), pltpu.VMEM(rows, bf16), pltpu.VMEM((width - main_rows, width), bf16),
            ],
        )(hidden_two_p, cot, mod, middle, up_w, up_w, down_w)

    share_forget, share_taps, share_bias = w_forget.shape[0], conv_taps.shape[0], b_ada.shape[0]

    if packed_here:
        grad_middle, gqkv, gmain, gout_main, grad_small, gleft, grad_gate, sums_two, g_up = backward_fused(
            heads,
            share_taps,
            (mod, run, runt, taken, given, gate_pre, states, value_rims, taps),
            (ghp_two, perm, middle, cot, branch, mixed_p, mix, attention_w, qkv, xp),
            (gup_main, gup_left),
        )
        grad_input, mod_all, g_query, g_key, g_value, g_out, grad_small = finish_fused(
            (mod, sums_two, ggate_two, grad_gate, forget_p), (attention_w, gqkv, perm, x, grad_middle),
            (gmain, gout_main, gleft), grad_small,
        )
        g_forget = grad_small[:36, :heads].reshape(-1)
        g_taps = lax.dynamic_slice(grad_small[36:40].reshape(-1), (lax.rem(me * share_taps, LANES),), (share_taps,))
        grad_bias = grad_small[40, :heads]
        mod_all = mod_all.reshape(devices, -1)[:, :mod_width]
        shares = [piece.reshape(-1) for piece in (g_query, g_key, g_value, g_out, g_up, g_down)]
    else:
        grad_middle, grad_mixed, grad_mix, gout_main, gout_left, sums_two = call(
            functools.partial(second_kernel, head_width),
            (
                sds(rows), sds(rows, bf16), sds(rows, bf16), sds((GROUPS, 32, width), bf16),
                sds((GROUPS, 16, width), bf16), sds((8, width)),
            ),
            "second_norm",
            grid=(1,),
            in_specs=[
                whole(rows), whole((width, width)), whole(rows), whole((8, width)), whole(rows), whole(rows), whole(rows),
                whole(rows), main_spec(lambda i: (0, 3, 0)), left_spec(lambda i: (0, 8, 0)),
            ],
            out_specs=[
                whole(rows), whole(rows), whole(rows), whole((GROUPS, 32, width)), whole((GROUPS, 16, width)),
                whole((8, width)),
            ],
            scratch_shapes=[pltpu.VMEM(rows, f32), pltpu.VMEM(rows, bf16), pltpu.VMEM((width, length), bf16)],
        )(ghp_two, perm, middle, mod, cot, branch, mixed_p, mix, attention_w, attention_w)

        back = state_call(qkv[0], grad_mix, taken, edges(grad_mixed))
        if ways == 2:
            back = jnp.stack([
                jnp.concatenate([back[1, :width], back[0, width:]]), jnp.concatenate([back[0, :width], back[1, width:]])
            ])
        leaving, grad_rims = joined_states(back, total, width, head_width)
        if ways == 2:
            leaving = leaving[::-1]

        gq_local, gk_local, gv_local, pair_rows, pair_cols = call(
            functools.partial(pairs_kernel, head_width, heads),
            (sds(rows), sds(rows), sds(rows), sds((2, length, LANES)), sds((2, heads, length))),
            "pairs",
            scratch_shapes=[pltpu.VMEM((2, length, length), bf16)],
        )(qkv, grad_mix, run, runt)
        if seq_count > 2:
            rows_through = jnp.sum(states.astype(f32) * leaving.astype(f32), axis=(0, 2))
            through = jnp.exp(total[:heads]) * jnp.sum(rows_through.reshape(heads, head_width), axis=1)
            through = jnp.pad(through, (0, LANES - heads)).reshape(1, LANES)
        else:
            through = jnp.zeros((1, LANES), f32)
        early = jnp.where(place == 0, jnp.ones((1, LANES), f32), 0.0)

        pad_scratch = pltpu.VMEM((length + 2 * GRID, width), bf16)
        gqkv, grad_gate, grad_conv, grad_bias = call(
            functools.partial(carry_kernel, head_width, ways),
            (sds((3,) + rows, bf16), sds((length, LANES), bf16), sds((16, width)), sds((1, LANES))),
            "carry",
            scratch_shapes=[pad_scratch, pad_scratch],
        )(
            qkv, grad_mix, gq_local, gk_local, gv_local, pair_rows, pair_cols, taken, given, gate_pre, states, leaving,
            through, early, grad_mixed, grad_rims, value_rims, taps,
        )
        gmain, gleft, gforget, ghp_one = call(
            weights_kernel,
            (sds((GROUPS, 96, width), bf16), sds((GROUPS, 16, width), bf16), sds((width, LANES)), sds(rows)),
            "weights",
            grid=(3,),
            in_specs=[
                whole(rows), pl.BlockSpec((1,) + rows, lambda j: (j, 0, 0)), whole((length, LANES)),
                whole((width, LANES)), main_spec(lambda j: (0, j, 0)), left_spec(lambda j: (0, 8, 0)),
                left_spec(lambda j: (0, 0, 0)),
            ],
            out_specs=[
                main_spec(lambda j: (0, j, 0)), left_spec(lambda j: (0, 0, 0)), whole((width, LANES)), whole(rows),
            ],
            scratch_shapes=[pltpu.VMEM((width, length), bf16)],
        )(xp, gqkv, grad_gate, forget_p, attention_w, attention_w, gout_left)
        grad_input, sums_one = call(
            last_part, (sds(rows), sds((8, width))), "last_norm", scratch_shapes=[pltpu.VMEM(rows, f32)]
        )(ghp_one, perm, x, mod, grad_middle)

        gforget = gforget[:, :heads]
        gforget = jnp.concatenate(
            [gforget[:main_rows].reshape(GROUPS, 32, heads), gforget[main_rows:].reshape(GROUPS, 4, heads)], axis=1
        )
        grad_small = jnp.concatenate([gforget.reshape(devices, -1), grad_conv[:10].reshape(devices, -1)], axis=1)
        grad_small = lax.psum_scatter(grad_small, everywhere, scatter_dimension=0, tiled=True).reshape(-1)
        g_forget, g_taps = grad_small[:share_forget], grad_small[share_forget:]
        grad_bias = lax.psum(grad_bias[0, :heads], everywhere)
        grads = [
            jnp.concatenate([gmain, gout_main, gleft], axis=1), jnp.concatenate([gup_main, gup_left], axis=1),
            gdown.reshape(GROUPS, -1, width),
        ]
        shares = [
            lax.psum_scatter(g.reshape(-1), everywhere, scatter_dimension=0, tiled=True).astype(f32)
            for g in unpack_blocks(grads)
        ]
        grad_mod = jnp.concatenate([sums_one[:2], sums_two[2:3], sums_two[:2], ggate_two])
        mod_all = lax.all_gather(grad_mod.reshape(1, mod_width), everywhere, axis=0, tiled=True)

    mod_all = jnp.sum(mod_all.reshape(data_count, seq_count, mod_width), axis=1)
    grad_ada = jnp.dot(cond_part.astype(f32).T, mod_all, precision=lax.Precision.HIGHEST).reshape(-1)
    if inset is not None:
        grad_ada = lax.dynamic_slice(grad_ada, (inset,), (share,))
    grad_ada_bias = lax.dynamic_slice(jnp.sum(mod_all, axis=0), (me * share_bias,), (share_bias,))
    g_query, g_key, g_value, g_out, g_up, g_down = shares
    return (
        output[None], grad_input[None], grad_ada, grad_ada_bias, g_query, g_key, g_value, g_forget,
        grad_bias, g_taps, g_out, g_up, g_down,
    )


def solution(mesh):
    rows = P("dp", "seq", None)
    shard = P(("dp", "seq"))
    return jax.shard_map(
        on_device,
        mesh=mesh,
        in_specs=(
            rows, P("dp", None), rows, shard, shard, shard, shard, shard, shard, P(), shard, shard, shard, shard,
        ),
        out_specs=(
            rows, rows, shard, shard, shard, shard, shard, shard, P(), shard, shard, shard, shard,
        ),
        check_vma=False,
    )
```

time: 3390 us -> 398 us (0.12); the launches traced: 3350 us -> 394 us
  waiting for transfers between devices: 1350 us -> 0 us
  local copies, waits for them, and re-layouts: 926 us -> 18.3 us
  matrix products: 586 us -> 0.73 us
  Pallas kernels: 0 us -> 368 us
  other arithmetic: 318 us -> 5.91 us
  blocking collectives: 138 us -> 0 us
    unnamed x23 -> x0, waiting for transfers between devices: 936 us -> none
    dot_general x268 -> x1, matrix products: 586 us -> 0.73 us  [on_device(): jnp.dot(cond_part.astype(f32).T, mod_all, precision=lax.Precision.HIGHEST)]
    pallas_call x0 -> x4, Pallas kernels: none -> 368 us  [the longest x1 115 us: forward_fused(): pl.pallas_call(functools.partial(forward_kernel, head_width, heads, taps_...]
    all_gather x7 -> x0, waiting for transfers between devices: 300 us -> none  [the longest x1 92 us: on_device(): lax.all_gather(shards[0], ('dp', 'seq'), axis=0, tiled=True)]
    rev x9 -> x0, local copies, waits for them, and re-layouts: 251 us -> none  [reverse_rows(): return jnp.flip(tensor, axis=1)]
    all_gather x4 -> x0, other arithmetic: 195 us -> none  [the longest x1 49.1 us: on_device(): lax.all_gather(shards[4], ('dp', 'seq'), axis=0, tiled=True)]
    reshape x23 -> x6, local copies, waits for them, and re-layouts: 144 us -> 4.58 us  [the longest x1 1.58 us: on_device(): ada_part = w_ada.reshape(ada_rows, mod_width)]
    convert_element_type x27 -> x0, local copies, waits for them, and re-layouts: 136 us -> none  [the longest x2 32.8 us: on_device(): sectioned(grad_ada.reshape(-1)).astype(jnp.bfloat16)]
  transfers between devices with their start and end apart: 24 -> 0, of which waited for: 11 -> 0; matrix products, arithmetic and copies ran while one was open for 46% -> 0% of each run, Pallas kernels for 0% -> 0%
where the time goes in v1:
time: 398 us; the launch traced here: 394 us
  Pallas kernels  368 us (92%)
  local copies, waits for them, and re-layouts  18.3 us (5%)
  other arithmetic  5.91 us (1%)
    pallas_call x1, Pallas kernels, forward_fused(): pl.pallas_call(functools.partial(forward_kernel, head_width, heads, taps_...  115 us
    pallas_call x1, Pallas kernels, feed_fused(): pl.pallas_call(feed_fused_kernel, out_shape=(gathered_shape(own), sds(row...  105 us
    pallas_call x1, Pallas kernels, backward_fused(): pl.pallas_call(functools.partial(backward_kernel, head_width, heads, taps...  87.7 us
    pallas_call x1, Pallas kernels, finish_fused(): pl.pallas_call(finish_kernel, out_shape=(sds(rows), gathered_shape(own))...  59.5 us
    unnamed x25, local copies, waits for them, and re-layouts  10.2 us

profile of v1, /device:TPU:0, one launch (start us, length us, event | category | flops | bytes accessed | tf_op | source)
XLA Modules:
  0.0 393.5 jit_solution(8217494667489518427)
XLA Ops:
  0.7 1.2 bitcast_convert_fusion.bf_ref
  1.8 0.7 broadcast_in_dim.16
  2.5 0.9 dynamic_update_slice.7
  3.4 0.7 reduce.2
  4.1 0.8 reshape.125
  4.8 0.6 fusion.12.own_s
  5.5 0.2 dynamic_update_slice.6
  5.7 1.6 reshape.121
  7.2 1.4 fusion.2.ada_ref
  8.6 115.2 %forward.1 = (bf16[4,2,2,2,80,128]{5,4,3,2,1,0:T(8,128)(2,1)}, bf16[4,2,2,2,144,1152]{5,4,3,2,1,0:T(8,128)(2,1)}, bf16[4,2,2,2,144,1152]{5,4,3,2,1,0:T(8,128)(2,...) custom-call(bf16[512,1152]{1,0:T(8,128)(2,1)} %bitcast.61, ...), custom_call_target="tpu_custom_call" | custom-call | tf_op jit(solution)/shard_map/forward/pallas_call | solution.py:1228
  123.8 0.9 slice_convert_fusion
  124.7 105.3 %feed.1 = (bf16[4,2,2,2,144,1152]{5,4,3,2,1,0:T(8,128)(2,1)}, bf16[512,1152]{1,0:T(8,128)(2,1)}, f32[512,1152]{1,0:T(8,128)}, bf16[32,128,1152]{2,1,0:T(8,128)(2...) custom-call(bf16[512,1152]{1,0:T(8,128)(2,1)} %get-tuple-element.56.h2p, ...), custom_call_target="tpu_custom_call" | custom-call | tf_op jit(solution)/shard_map/feed/pallas_call | solution.py:1377
  230.0 87.7 %backward.1 = (f32[512,1152]{1,0:T(8,128)}, bf16[3,512,1152]{2,1,0:T(8,128)(2,1)}, bf16[32,96,1152]{2,1,0:T(8,128)(2,1)}, bf16[32,32,1152]{2,1,0:T(8,128)(2,1)},...) custom-call(f32[8,1152]{1,0:T(8,128)} %get-tuple-element.57.mod_ref,, ...), custom_call_target="tpu_custom_call" | custom-call | tf_op jit(solution)/shard_map/backward/pallas_call | solution.py:1572
  317.7 59.5 %finish.1 = (f32[512,1152]{1,0:T(8,128)}, f32[4,2,2,2,64,128]{5,4,3,2,1,0:T(8,128)}, f32[324,128]{1,0:T(8,128)}, f32[324,128]{1,0:T(8,128)}, f32[324,128]{1,0:T(...) custom-call(f32[8,1152]{1,0:T(8,128)} %get-tuple-element.57.mod_ref, f32[8,1152]{1,0:T(8,128)} %get-tuple-element.79.sums_two, ...), custom_call_target="tpu_custom_call" | custom-call | tf_op jit(solution)/shard_map/finish/pallas_call | solution.py:1667
  377.2 1.8 copy.33
  379.0 0.1 slice_reduce_fusion
  379.1 0.6 dynamic_slice.10
  379.8 0.5 slice_bitcast_fusion.1
  380.3 0.7 reshape.147
  381.0 0.6 dynamic_slice.11
  381.6 0.5 reshape.142
  382.1 1.0 reduce_sum.18
  383.2 0.7 fusion.13
  383.9 1.0 reshape.143
  385.0 2.4 copy.44
  387.4 1.4 copy.45
  388.8 0.7 copy.46
  389.5 0.7 copy.47
  390.2 0.7 copy.48
  390.9 0.7 copy.49
  391.5 0.9 copy.50
  392.4 0.9 copy.51
  (21 shorter events, 0.1 us)
Async XLA Ops:
  377.2 2.6 copy-start.7
  383.9 3.5 copy-start
  387.4 1.4 copy-start.6
  387.4 2.1 copy-start.5
  387.4 2.8 copy-start.4
  387.4 3.5 copy-start.3
  387.4 4.2 %copy-start.2 = (f32[1296,128]{1,0:T(8,128)S(1)}, f32[1296,128]{1,0:T(8,128)}, u32[]{:S(2)}) copy-start(f32[1296,128]{1,0:T(8,128)} %get-tuple-element.97) | copy-start | bytes 1990660
  388.8 3.6 copy-start.1
